TPU v7x, 128 devices: a whole 4x4x4 slice. The times are simulated.
128 devices in a mesh: ctx: 32 (over x, y_lo, z), tp: 4 (over y_hi, core).
Axes of the slice: x: 4, y: 4 (y_hi: 2, y_lo: 2; y = y_hi * 2 + y_lo), z: 4, core: 2. Of those that a mesh axis runs over, the one named last changes fastest.
Arguments:
- stream_in: bfloat16 [4096, 6144], P(('ctx', 'tp')), may hold values from -3 to 3
- queries: bfloat16 [4096, 3072], P('ctx', 'tp'), may hold values from -5 to 5
- rotated_key_heads: bfloat16 [4096, 512], P('ctx', 'tp'), may hold values from -5 to 5
- values: bfloat16 [4096, 512], P('ctx', 'tp'), may hold values from -6 to 6
- doc_ids: int32 [4096], P('ctx'), may hold values from 0 to 7, never falling along the last dimension, each value on 1 to 2048 neighbouring positions
- out_proj: bfloat16 [3072, 6144], P('tp', 'ctx'), may hold values from -0.4375 to 0.4375
- norm_gain: float32 [6144], replicated, may hold values from 0.1 to 1.9
- router: float32 [6144, 8], replicated, may hold values from -0.078125 to 0.078125
- w_gate: bfloat16 [6144, 65536], P(None, ('ctx', 'tp')), may hold values from -0.078125 to 0.078125
- w_up: bfloat16 [6144, 65536], P(None, ('ctx', 'tp')), may hold values from -0.078125 to 0.078125
- w_down: bfloat16 [65536, 6144], P(('ctx', 'tp')), may hold values from -0.0625 to 0.0625
- routes: int32 [4096, 2], P(('ctx', 'tp')), may hold values from 0 to 7, all different within a row; in each aligned block of 32 rows (0 to 31, 32 to 63, ...) at most 9 rows name the same one
Outputs:
- layer_out: bfloat16 [4096, 6144], P(('ctx', 'tp'))
Inputs may be any that keep to these rules, and one draw needn't show every extreme that they name: `doc_ids`: starts at 0 and never falls; each document holds 1 to 2048 positions, and one holds exactly 2048. `routes`: each row names two different experts; in each aligned block of 32 rows (the rows of one device) no expert is named by more than 9 rows, and in every draw some block names some expert exactly 9 times.
All inputs are finite; a program needn't handle non-finite values.
Results may differ from a plain program's by a relative error of at most 0.019.
Values may be sent and summed in bfloat16 or wider, within the bound.
No kernel may reach another device: no remote copies, remote signals or barrier semaphores. Data moves between devices by JAX's collectives and lax.ppermute only.
A program may use at most 192 MiB of HBM per device.

v0:
```python
import functools

import jax
import jax.numpy as jnp
from jax import lax
from jax.experimental import pallas as pl
from jax.experimental.pallas import tpu as pltpu
from jax.sharding import Mesh, PartitionSpec as P

HEAD_WIDTH = 128
NX, NYL, NZ, NYH, NC = 4, 2, 4, 2, 2
SWAP = [(0, 1), (1, 0)]
UP = [(i, (i + 1) % NZ) for i in range(NZ)]
DOWN = [((i + 1) % NZ, i) for i in range(NZ)]


def add(*terms):
    total = terms[0].astype(jnp.float32)
    for term in terms[1:]:
        total = total + term.astype(jnp.float32)
    return total.astype(jnp.bfloat16)


def after(value, *others):
    return lax.optimization_barrier((value, *others))[0]


def from_behind(array, back, flip):
    route = [
        (x * NYL + yl, (x + back) * NYL + (yl ^ flip)) for x in range(NX - back) for yl in range(NYL)
    ]
    return lax.ppermute(array, ("x", "yl"), route)


def gather_keys(keys, values, doc_ids):
    tok = keys.shape[0]
    docs = jnp.pad(doc_ids.astype(jnp.bfloat16)[None, :], ((0, 15), (0, 0)))
    own = jnp.concatenate([keys, values, docs], axis=0)
    order = [(flip, back) for flip in range(NYL) for back in range(3)]
    pieces = [from_behind(own, back, flip) if flip or back else own for flip, back in order]
    here = jnp.concatenate(pieces, axis=0)
    below = lax.ppermute(here, "z", UP)
    above = lax.ppermute(here, "z", DOWN)
    half = here.shape[0] // 2
    far_first = lax.ppermute(below[:half], "z", UP)
    far_second = lax.ppermute(above[half:], "z", DOWN)
    x, yl, z = lax.axis_index("x"), lax.axis_index("yl"), lax.axis_index("z")
    at_x = x - jnp.arange(3, dtype=jnp.int32)
    at_yl = jnp.stack([yl, 1 - yl])
    at_z = (z + jnp.array([0, 3, 1, 2], jnp.int32)) % NZ
    base = (at_x[None, None, :] * NYL + at_yl[None, :, None]) * NZ + at_z[:, None, None]
    base = jnp.where(at_x[None, None, :] >= 0, base * tok, 1 << 30).reshape(-1)
    own_base = ((x * NYL + yl) * NZ + z) * tok
    return (here, below, above, far_first, far_second), jnp.append(base, own_base)


def attention_kernel(base, query, query_doc, here, below, above, far_a, far_b, out, *scratch):
    rows, keys, vals, bias, scores, peak, total, accum = scratch
    tok = query.shape[0]
    heads = query.shape[1] // HEAD_WIDTH
    width = HEAD_WIDTH
    step = here.shape[0] // 6
    blocks = [(ref, i * step) for ref in (here, below, above) for i in range(6)]
    blocks += [(ref, i * step) for ref in (far_a, far_b) for i in range(3)]
    count = len(blocks)
    wide = 4 * tok
    for h in range(heads):
        rows[h * tok : (h + 1) * tok] = query[:, h * width : (h + 1) * width]
    query_at = base[count] + lax.broadcasted_iota(jnp.int32, (tok, tok), 0)
    lane = lax.broadcasted_iota(jnp.int32, (tok, tok), 1)
    for i, (ref, first) in enumerate(blocks):
        keys[i * tok : (i + 1) * tok] = ref[first : first + tok]
        vals[i * tok : (i + 1) * tok] = ref[first + tok : first + 2 * tok]
        docs = ref[first + 2 * tok : first + step].astype(jnp.float32)[0:1]
        allowed = (docs == query_doc[...]) & (base[i] + lane <= query_at)
        bias[i // 4, :, (i % 4) * tok : (i % 4 + 1) * tok] = jnp.where(allowed, 0.0, -1e30)
    peak[...] = jnp.full(peak.shape, -1e30, jnp.float32)
    total[...] = jnp.zeros_like(total)
    accum[...] = jnp.zeros_like(accum)

    def lanes(array):
        return [array[:, i * width : (i + 1) * width] for i in range(wide // width)]

    @pl.loop(0, count // 4)
    def _(i):
        at = pl.ds(pl.multiple_of(i * wide, wide), wide)
        value = lax.dot_general(
            rows[...], keys[at], (((1,), (1,)), ((), ())), preferred_element_type=jnp.float32
        )
        value = value.reshape(heads, tok, wide) * (width ** (-0.5)) + bias[i][None]
        value = value.reshape(heads * tok, wide)
        scores[i] = value
        peak[...] = functools.reduce(jnp.maximum, lanes(value), peak[...])

    top = jnp.max(peak[...], axis=1, keepdims=True)
    peak[...] = jnp.broadcast_to(top, peak.shape)

    @pl.loop(0, count // 4)
    def _(i):
        at = pl.ds(pl.multiple_of(i * wide, wide), wide)
        expo = jnp.exp(scores[i] - jnp.concatenate([peak[...]] * (wide // width), axis=1))
        total[...] = functools.reduce(jnp.add, lanes(expo), total[...])
        accum[...] += jnp.dot(
            expo.astype(jnp.bfloat16), vals[at], preferred_element_type=jnp.float32
        )

    result = accum[...] / jnp.sum(total[...], axis=1, keepdims=True)
    for h in range(heads):
        out[:, h * width : (h + 1) * width] = result[h * tok : (h + 1) * tok].astype(out.dtype)


def attention(queries, keys, values, doc_ids):
    tok, columns = queries.shape
    heads = columns // HEAD_WIDTH
    arrays, base = gather_keys(keys, values, doc_ids)
    whole = pl.BlockSpec(memory_space=pltpu.VMEM)
    return pl.pallas_call(
        attention_kernel,
        in_specs=[pl.BlockSpec(memory_space=pltpu.SMEM)] + [whole] * 7,
        out_specs=whole,
        out_shape=jax.ShapeDtypeStruct(queries.shape, jnp.bfloat16),
        scratch_shapes=[
            pltpu.VMEM((heads * tok, HEAD_WIDTH), jnp.bfloat16),
            pltpu.VMEM((24 * tok, HEAD_WIDTH), jnp.bfloat16),
            pltpu.VMEM((24 * tok, HEAD_WIDTH), jnp.bfloat16),
            pltpu.VMEM((6, tok, 4 * tok), jnp.float32),
            pltpu.VMEM((6, heads * tok, 4 * tok), jnp.float32),
            pltpu.VMEM((heads * tok, HEAD_WIDTH), jnp.float32),
            pltpu.VMEM((heads * tok, HEAD_WIDTH), jnp.float32),
            pltpu.VMEM((heads * tok, HEAD_WIDTH), jnp.float32),
        ],
        compiler_params=pltpu.CompilerParams(vmem_limit_bytes=40 * 1024 * 1024),
        cost_estimate=pl.CostEstimate(
            flops=4 * heads * tok * 24 * tok * HEAD_WIDTH,
            bytes_accessed=4 * 24 * tok * HEAD_WIDTH,
            transcendentals=heads * tok * 24 * tok,
        ),
        name="attention",
    )(base, queries, doc_ids.astype(jnp.float32)[:, None], *arrays), arrays[0]


def gather_projection(out_proj):
    own = out_proj.T
    other = lax.ppermute(own, "yl", SWAP)
    first = lax.axis_index("yl") == 0
    pair = jnp.concatenate([jnp.where(first, own, other), jnp.where(first, other, own)], axis=0)
    return lax.all_gather(pair, "x", axis=0, tiled=True)


def project(heads_out, weight):
    tok = heads_out.shape[0]
    width = weight.shape[0]
    depth = width // (NX * NYL)
    rows = tok // (NYH * NC)
    spread = jnp.broadcast_to(heads_out[None], (NZ,) + heads_out.shape)
    all_z = lax.all_to_all(spread, "z", split_axis=0, concat_axis=0, tiled=True)
    part = lax.dot_general(
        all_z.reshape(NZ * tok, -1),
        weight,
        (((1,), (1,)), ((), ())),
        preferred_element_type=jnp.float32,
    ).astype(jnp.bfloat16)
    part = part.reshape(NZ, NYH, NC, rows, width)
    c = lax.axis_index("c")
    got = lax.ppermute(lax.dynamic_index_in_dim(part, 1 - c, 2, False), "c", SWAP)
    part = add(lax.dynamic_index_in_dim(part, c, 2, False), got)
    part = lax.all_to_all(
        part.reshape(NZ * NYH, rows, width), ("z", "yh"), split_axis=0, concat_axis=0, tiled=True
    )
    part = part.reshape(NZ, NYH, rows, NX * NYL, depth)
    total = part[:, 0].astype(jnp.float32) + part[:, 1].astype(jnp.float32)
    return total.transpose(1, 2, 0, 3).reshape(rows, NX * NYL * NZ * depth)


def expert_kernel(count, core_ref, *refs):
    own, other = refs[:count], refs[count : 2 * count]
    gate_w, up_w, down_w = refs[2 * count : 2 * count + 3]
    send, keep = refs[2 * count + 3 : 3 * count + 3], refs[3 * count + 3 : 4 * count + 3]
    gate_sum, up_sum, hidden = refs[4 * count + 3 :]
    step = pl.program_id(0)
    high = own[0].shape[0]

    def contract(parts, first):
        rows = jnp.concatenate([part[...] for part in parts], axis=0)
        gate = jnp.dot(rows, gate_w[...], preferred_element_type=jnp.float32)
        up = jnp.dot(rows, up_w[...], preferred_element_type=jnp.float32)
        if first:
            gate_sum[...], up_sum[...] = gate, up
        else:
            gate_sum[...] += gate
            up_sum[...] += up

    def expand(outs):
        value = jnp.dot(hidden[...], down_w[...], preferred_element_type=jnp.float32)
        for i, out in enumerate(outs):
            out[...] = value[i * high : (i + 1) * high].astype(out.dtype)

    @pl.when(step == 0)
    def _():
        contract(own, True)

    @pl.when(step == 1)
    def _():
        contract(own, False)

    @pl.when((step == 2) | (step == 3))
    def _():
        contract(other, False)

    @pl.when(step == 3)
    def _():
        gate = gate_sum[...]
        hidden[...] = (gate / (1.0 + jnp.exp(-gate)) * up_sum[...]).astype(hidden.dtype)

    @pl.when((step == 4) | (step == 5))
    def _():
        expand(send)

    @pl.when(step >= 6)
    def _():
        expand(keep)


def expert_part(core, own, other, w_gate, w_up, w_down):
    count = len(own)
    high, half = own[0].shape
    quarter = half // 2
    units = w_gate.shape[1]

    def place(first):
        return pl.BlockSpec((high, quarter), lambda s, c: (0, jnp.clip(s - first, 0, 1)))

    def in_quarter(s, c):
        s = jnp.minimum(s, 3)
        return jnp.where(s < 2, 2 * c[0] + s, 2 * (1 - c[0]) + s - 2)

    def out_quarter(s, c):
        s = jnp.maximum(s, 4) - 4
        return jnp.where(s < 2, 2 * (1 - c[0]) + s, 2 * c[0] + s - 2)

    rows = count * high
    outs = pl.pallas_call(
        functools.partial(expert_kernel, count),
        grid_spec=pltpu.PrefetchScalarGridSpec(
            num_scalar_prefetch=1,
            grid=(8,),
            in_specs=[place(0)] * count
            + [place(2)] * count
            + [
                pl.BlockSpec((quarter, units), lambda s, c: (in_quarter(s, c), 0)),
                pl.BlockSpec((quarter, units), lambda s, c: (in_quarter(s, c), 0)),
                pl.BlockSpec((units, quarter), lambda s, c: (0, out_quarter(s, c))),
            ],
            out_specs=[place(4)] * count + [place(6)] * count,
            scratch_shapes=[
                pltpu.VMEM((rows, units), jnp.float32),
                pltpu.VMEM((rows, units), jnp.float32),
                pltpu.VMEM((rows, units), jnp.bfloat16),
            ],
        ),
        out_shape=[jax.ShapeDtypeStruct((high, half), jnp.bfloat16)] * (2 * count),
        compiler_params=pltpu.CompilerParams(vmem_limit_bytes=48 * 1024 * 1024),
        cost_estimate=pl.CostEstimate(
            flops=6 * rows * 2 * half * units,
            bytes_accessed=12 * half * units + 8 * rows * half,
            transcendentals=rows * units,
        ),
        name="expert_part",
    )(core, *own, *other, w_gate, w_up, w_down)
    return outs[:count], outs[count:]


def experts_of(own, w_gate, w_up, w_down):
    cut = own.shape[0] // 32 * 16
    c = lax.axis_index("c").astype(jnp.int32).reshape(1)

    def run(*blocks):
        other = [lax.ppermute(block, "c", SWAP) for block in blocks]
        return expert_part(c, blocks, other, w_gate, w_up, w_down)

    def summed(parts):
        send, keep = parts
        return [add(mine, lax.ppermute(his, "c", SWAP)) for mine, his in zip(keep, send)]

    def near(block):
        return lax.ppermute(block, "z", UP), lax.ppermute(block, "z", DOWN)

    def near_back(below, above):
        return lax.ppermute(below, "z", DOWN), lax.ppermute(above, "z", UP)

    rest = own.shape[0] - cut
    over = lax.ppermute(own, "yh", SWAP)
    below, above = near(own)
    up = lax.ppermute(jnp.concatenate([below[:cut], over], axis=0), "z", UP)
    down = lax.ppermute(jnp.concatenate([above[cut:], over], axis=0), "z", DOWN)
    far_own = jnp.concatenate([up[:cut], down[:rest]], axis=0)
    over_below, over_above = up[cut:], down[rest:]
    far_over = lax.ppermute(far_own, "yh", SWAP)
    own, over, below, above = summed(run(own, over, below, above))
    own_back = near_back(below, above)
    parts = run(after(far_own, own, over, below, above), over_below, over_above)
    far_over = after(far_over, *own_back, parts[1][-1])
    last = run(far_over)
    far_own, over_below, over_above = summed(parts)
    over_back = near_back(over_below, over_above)
    (far_over,) = summed(last)
    far_own = add(far_own, lax.ppermute(far_over, "yh", SWAP))
    over = lax.ppermute(add(over, *over_back), "yh", SWAP)
    far_own = lax.ppermute(after(far_own, *over_back), "z", [(i, (i + 2) % NZ) for i in range(NZ)])
    return add(own, *own_back, far_own, over)


def per_device(
    stream_in,
    queries,
    rotated_key_heads,
    values,
    doc_ids,
    out_proj,
    norm_gain,
    router,
    w_gate,
    w_up,
    w_down,
    routes,
):
    heads_out, gathered = attention(queries, rotated_key_heads, values, doc_ids)
    summed = project(heads_out, gather_projection(after(out_proj, gathered)))
    resid = stream_in.astype(jnp.float32) + summed.astype(jnp.float32)
    width = resid.shape[1]
    normed = (
        resid * lax.rsqrt(jnp.mean(resid * resid, axis=1, keepdims=True) + 1e-05) * norm_gain
    ).astype(jnp.bfloat16)
    logits = jnp.dot(normed.astype(jnp.float32), router, precision=lax.Precision.HIGHEST)
    experts = router.shape[1]
    rows = normed.shape[0]
    cap = 2 * rows * 9 // 32
    slots = experts * cap
    c = lax.axis_index("c")
    half = width // 2

    def columns(array, core):
        return lax.dynamic_slice_in_dim(array, core * half, half, axis=1)

    def in_order(mine, his, axis):
        return jnp.where(
            c == 0,
            jnp.concatenate([mine, his], axis=axis),
            jnp.concatenate([his, mine], axis=axis),
        )

    pair_routes = in_order(routes, lax.ppermute(routes, "c", SWAP), 0)
    pair_normed = in_order(columns(normed, c), lax.ppermute(columns(normed, 1 - c), "c", SWAP), 0)
    rows2 = 2 * rows
    hits = pair_routes[:, :, None] == jnp.arange(experts, dtype=jnp.int32)
    flat_hits = hits.astype(jnp.int32).reshape(rows2 * 2, experts)
    before = jnp.cumsum(flat_hits, axis=0) - flat_hits
    slot = jnp.sum(before.reshape(rows2, 2, experts) * hits.astype(jnp.int32), axis=-1)
    target = pair_routes * cap + slot
    placed = target[:, :, None] == jnp.arange(slots, dtype=jnp.int32)[None, None, :]
    chooser = jnp.any(placed, axis=1).astype(jnp.bfloat16).T
    own_hits = routes[:, :, None] == jnp.arange(experts, dtype=jnp.int32)
    pair_logits = jnp.sum(jnp.where(own_hits, logits[:, None, :], 0.0), axis=-1)
    first_gate = 1.0 / (1.0 + jnp.exp(pair_logits[:, 1] - pair_logits[:, 0]))
    second_gate = 1.0 / (1.0 + jnp.exp(pair_logits[:, 0] - pair_logits[:, 1]))
    own_gates = jnp.stack([first_gate, second_gate], axis=1)
    gate_pair = in_order(own_gates, lax.ppermute(own_gates, "c", SWAP), 0)
    combiner = jnp.sum(jnp.where(placed, gate_pair[:, :, None], 0.0), axis=1)

    packed = jnp.dot(chooser, pair_normed, preferred_element_type=jnp.float32).astype(jnp.bfloat16)
    arrived = lax.all_to_all(
        packed.reshape(experts, cap, half), ("x", "yl"), split_axis=0, concat_axis=0, tiled=True
    ).reshape(slots, half)
    home = experts_of(arrived, w_gate, w_up, w_down)
    returned = lax.all_to_all(
        home.reshape(experts, cap, half), ("x", "yl"), split_axis=0, concat_axis=0, tiled=True
    ).reshape(slots, half)
    mixture = jnp.dot(combiner, returned.astype(jnp.float32), precision=lax.Precision.HIGHEST)
    mine = lax.dynamic_slice_in_dim(mixture, c * rows, rows, axis=0)
    his = lax.dynamic_slice_in_dim(mixture, (1 - c) * rows, rows, axis=0)
    mixture = in_order(mine, lax.ppermute(his, "c", SWAP), 1)
    return (resid + mixture).astype(jnp.bfloat16)


def solution(mesh):
    fine = Mesh(mesh.devices.reshape(NX, NYL, NZ, NYH, NC), ("x", "yl", "z", "yh", "c"))
    ctx, tp = ("x", "yl", "z"), ("yh", "c")
    placed = (
        P(ctx + tp, None),
        P(ctx, tp),
        P(ctx, tp),
        P(ctx, tp),
        P(ctx),
        P(tp, ctx),
        P(),
        P(),
        P(None, ctx + tp),
        P(None, ctx + tp),
        P(ctx + tp, None),
        P(ctx + tp, None),
    )
    return jax.shard_map(
        per_device, mesh=fine, in_specs=placed, out_specs=P(ctx + tp, None), check_vma=False
    )
```

profile of v0, /device:TPU:1, one launch (start us, length us, event | category | flops | bytes accessed | tf_op | source)
XLA Modules:
  0.0 326.6 jit_solution(17875498406198065916)
XLA Ops:
  9.6 3.9 %collective-permute-start = (bf16[272,128]{1,0:T(8,128)(2,1)S(1)}, bf16[272,128]{1,0:T(8,128)(2,1)S(1)}, u32[]{:S(2)}, u32[]{:S(2)}) collective-permute-start(bf16[272,128]{1,0:T(8,128)(2,1)S(1)} %pad_maximum_fusion.4), channel_id=1, source_target_pairs={{0,32},{16,48},{32,64},{48,80},{64,96},{80,112},{1,33},{17,49},{33... | collective-permute-start | bytes 208904 | tf_op jit(solution)/shard_map/ppermute | solution.py:32
  13.5 4.4 %collective-permute-start.1 = (bf16[272,128]{1,0:T(8,128)(2,1)S(1)}, bf16[272,128]{1,0:T(8,128)(2,1)S(1)}, u32[]{:S(2)}, u32[]{:S(2)}) collective-permute-start(bf16[272,128]{1,0:T(8,128)(2,1)S(1)} %pad_maximum_fusion.4), channel_id=1, source_target_pairs={{0,64},{16,80},{32,96},{48,112},{1,65},{17,81},{33,97},{49,113},{2... | collective-permute-start | bytes 208904 | tf_op jit(solution)/shard_map/ppermute | solution.py:32
  17.9 1.4 collective-permute-start.2
  19.3 1.3 collective-permute-start.3
  20.6 2.2 collective-permute-start.4
  22.9 1.3 collective-permute-done.4
  25.1 6.0 %collective-permute-done.9 = bf16[192,768]{1,0:T(8,128)(2,1)S(1)} collective-permute-done((bf16[192,768]{1,0:T(8,128)(2,1)}, bf16[192,768]{1,0:T(8,128)(2,1)S(1)}, u32[]{:S(2)}, u32[]{:S(2)}) %collective-permute-start.9) | collective-permute-done | bytes 294944 | tf_op jit(solution)/shard_map/ppermute | solution.py:144
  31.1 1.0 broadcast_select_fusion.1
  33.1 1.6 collective-permute-start.5
  34.7 2.2 collective-permute-start.6
  37.0 6.9 %collective-permute-done.5.below = bf16[1632,128]{1,0:T(8,128)(2,1)S(1)} collective-permute-done((bf16[1632,128]{1,0:T(8,128)(2,1)S(1)}, bf16[1632,128]{1,0:T(8,128)(2,1)S(1)}, u32[]{:S(2)}, u32[]{:S(2)}) %collective-permute-start.5) | collective-permute-done | bytes 417824 | tf_op jit(solution)/shard_map/ppermute | solution.py:42
  44.1 2.7 collective-permute-start.8
  47.1 2.7 collective-permute-done.7.far_a
  49.9 6.2 %attention.1 = bf16[128,768]{1,0:T(8,128)(2,1)S(1)} custom-call(s32[25]{0:T(128)S(1)} %pad_add_fusion.3.base, bf16[128,768]{1,0:T(8,128)(2,1)S(1)} %copy-done.1, f32[128,1]{1,0:T(8,128)S(1)} %copy.40.query_doc, bf16[1632,128]{1,0:T(8,128)(2,1)S(1)} %constant_dynamic-update-slice_fusion.here, bf16[1632,128]{1,0:T(8,128)(2,1)S(1)} %collective-permute-done.5.below, ...), custom_call_target="tpu_custom_call" | custom-call | flops 1207959552 | bytes 1572864 | tf_op jit(solution)/shard_map/attention/pallas_call | solution.py:117
  57.0 4.0 %all-to-all-start = ((bf16[4,128,768]{2,1,0:T(8,128)(2,1)}), bf16[4,128,768]{2,1,0:T(8,128)(2,1)S(1)}, u32[]{:S(2)}, u32[]{:S(2)}) async-start(bf16[4,128,768]{2,1,0:T(8,128)(2,1)} %broadcast_in_dim.66), calls=%async_computation | async-start | bytes 1572864 | tf_op jit(solution)/shard_map/all_to_all | solution.py:156
  61.0 8.4 %all-to-all-done = bf16[4,128,768]{2,1,0:T(8,128)(2,1)S(1)} async-done(((bf16[4,128,768]{2,1,0:T(8,128)(2,1)}), bf16[4,128,768]{2,1,0:T(8,128)(2,1)S(1)}, u32[]{:S(2)}, u32[]{:S(2)}) %all-to-all-start) | async-done | bytes 786464 | tf_op jit(solution)/shard_map/all_to_all | solution.py:156
  69.4 2.0 all-gather.2.cloned.1.call-done
  71.5 3.1 convolution_convert_fusion.1
  74.6 4.4 %collective-permute-start.10 = (bf16[4,2,32,1536]{3,2,1,0:T(8,128)(2,1)S(1)}, bf16[4,2,32,1536]{3,2,1,0:T(8,128)(2,1)S(1)}, u32[]{:S(2)}, u32[]{:S(2)}) collective-permute-start(bf16[4,2,32,1536]{3,2,1,0:T(8,128)(2,1)S(1)} %dynamic-slice_bitcast_fusion), channel_id=1, source_target_pairs={{0,1},{1,0},{2,3},{3,2},{4,5},{5,4},{6,7},{7,6},{8,9},{9,8},{10,11... | collective-permute-start | bytes 2359304 | tf_op jit(solution)/shard_map/ppermute | solution.py:165
  79.0 1.9 collective-permute-done.10
  80.9 1.1 fusion
  82.0 4.5 %all-to-all-start.1 = ((bf16[8,32,1536]{2,1,0:T(8,128)(2,1)}), bf16[8,32,1536]{2,1,0:T(8,128)(2,1)S(1)}, u32[]{:S(2)}, u32[]{:S(2)}) async-start(bf16[8,32,1536]{2,1,0:T(8,128)(2,1)} %bitcast.10), calls=%async_computation.1 | async-start | bytes 1572864 | tf_op jit(solution)/shard_map/all_to_all | solution.py:167
  89.3 10.8 %all-to-all-done.1 = bf16[8,32,1536]{2,1,0:T(8,128)(2,1)S(1)} async-done(((bf16[8,32,1536]{2,1,0:T(8,128)(2,1)}), bf16[8,32,1536]{2,1,0:T(8,128)(2,1)S(1)}, u32[]{:S(2)}, u32[]{:S(2)}) %all-to-all-start.1) | async-done | bytes 786464 | tf_op jit(solution)/shard_map/all_to_all | solution.py:167
  103.2 1.9 collective-permute-start.13
  106.8 20.3 %all_to_all.20 = bf16[8,18,3072]{2,1,0:T(8,128)(2,1)S(1)} all-to-all(bf16[8,18,3072]{2,1,0:T(8,128)(2,1)S(1)} %reshape.206), channel_id=1, replica_groups=mesh['x'=4,'yl'=2,'z'=4,'yh'=2,'c'=2] {'x','yl'}, dimensions={0} | all-to-all | bytes 1769472 | tf_op jit(solution)/shard_map/all_to_all | solution.py:371
  127.2 1.2 reshape.207.refs_0_
  128.4 1.5 collective-permute-start.14
  130.4 2.4 collective-permute-start.16
  132.8 2.7 collective-permute-start.17
  135.5 13.6 %collective-permute-done.14.refs_1_ = bf16[144,3072]{1,0:T(8,128)(2,1)S(1)} collective-permute-done((bf16[144,3072]{1,0:T(8,128)(2,1)}, bf16[144,3072]{1,0:T(8,128)(2,1)S(1)}, u32[]{:S(2)}, u32[]{:S(2)}) %collective-permute-start.14) | collective-permute-done | bytes 884768 | tf_op jit(solution)/shard_map/ppermute | solution.py:292
  149.1 3.1 collective-permute-start.18
  152.2 1.4 collective-permute-start.19
  154.6 2.2 collective-permute-start.27
  157.8 1.0 copy-done.22
  158.8 19.1 %expert_part.3 = (bf16[144,3072]{1,0:T(8,128)(2,1)S(1)}, bf16[144,3072]{1,0:T(8,128)(2,1)S(1)}, bf16[144,3072]{1,0:T(8,128)(2,1)S(1)}, bf16[144,3072]{1,0:T(8,12...) custom-call(s32[1]{0:T(128)} %bitcast.15.core_ref, ...), custom_call_target="tpu_custom_call" | custom-call | flops 10871635968 | bytes 33030144 | tf_op jit(solution)/shard_map/expert_part/pallas_call | solution.py:242
  177.9 1.1 collective-permute-start.24
  179.5 4.8 %collective-permute-done.26 = bf16[208,3072]{1,0:T(8,128)(2,1)S(1)} collective-permute-done((bf16[208,3072]{1,0:T(8,128)(2,1)S(1)}, bf16[208,3072]{1,0:T(8,128)(2,1)S(1)}, u32[]{:S(2)}, u32[]{:S(2)}) %collective-permute-start.26) | collective-permute-done | bytes 1277984 | tf_op jit(solution)/shard_map/ppermute | solution.py:294
  184.3 1.3 collective-permute-start.21
  186.2 1.1 collective-permute-start.30
  187.6 1.1 copy-done.9
  189.8 1.6 collective-permute-start.33
  191.3 1.4 collective-permute-start.25
  192.8 11.9 %collective-permute-start.23 = (bf16[144,3072]{1,0:T(8,128)(2,1)S(1)}, bf16[144,3072]{1,0:T(8,128)(2,1)S(1)}, u32[]{:S(2)}, u32[]{:S(2)}) collective-permute-start(bf16[144,3072]{1,0:T(8,128)(2,1)S(1)} %add_convert_fusion.9), channel_id=1, source_target_pairs={{4,0},{8,4},{12,8},{0,12},{5,1},{9,5},{13,9},{1,13},{6,2},{10,6},{... | collective-permute-start | bytes 2654216 | tf_op jit(solution)/shard_map/ppermute | solution.py:289
  205.6 15.7 %expert_part.4 = (bf16[144,3072]{1,0:T(8,128)(2,1)S(1)}, bf16[144,3072]{1,0:T(8,128)(2,1)S(1)}, bf16[144,3072]{1,0:T(8,128)(2,1)S(1)}, bf16[144,3072]{1,0:T(8,12...) custom-call(s32[1]{0:T(128)} %bitcast.15.core_ref, ...), custom_call_target="tpu_custom_call" | custom-call | flops 8153726976 | bytes 29491200 | tf_op jit(solution)/shard_map/expert_part/pallas_call | solution.py:242
  221.3 1.6 collective-permute-done.23
  223.9 1.6 collective-permute-start.34
  225.9 1.5 collective-permute-done.34.refs_1_
  227.5 11.0 %expert_part.5 = (bf16[144,3072]{1,0:T(8,128)(2,1)S(1)}, bf16[144,3072]{1,0:T(8,128)(2,1)S(1)}) custom-call(s32[1]{0:T(128)} %bitcast.15.core_ref, bf16[144,3072]{1,0:T(8,128)(2,1)S(1)} %collective-permute-done.33.refs_0_, bf16[144,3072]{1,0:T(8,128)(2,1)S(1)} %collective-permute-done.34.refs_1_, bf16[6144,512]{1,0:T(8,128)(2,1)} %refs_2_.1, ...), custom_call_target="tpu_custom_call" | custom-call | flops 2717908992 | bytes 22413312 | tf_op jit(solution)/shard_map/expert_part/pallas_call | solution.py:242
  239.1 3.5 %collective-permute-start.38 = (bf16[144,3072]{1,0:T(8,128)(2,1)S(1)}, bf16[144,3072]{1,0:T(8,128)(2,1)S(1)}, u32[]{:S(2)}, u32[]{:S(2)}) collective-permute-start(bf16[144,3072]{1,0:T(8,128)(2,1)S(1)} %add_convert_fusion.3), channel_id=1, source_target_pairs={{4,0},{8,4},{12,8},{0,12},{5,1},{9,5},{13,9},{1,13},{6,2},{10,6},{... | collective-permute-start | bytes 2654216 | tf_op jit(solution)/shard_map/ppermute | solution.py:289
  243.6 1.5 collective-permute-start.36
  245.2 16.3 %collective-permute-done.38 = bf16[144,3072]{1,0:T(8,128)(2,1)S(1)} collective-permute-done((bf16[144,3072]{1,0:T(8,128)(2,1)S(1)}, bf16[144,3072]{1,0:T(8,128)(2,1)S(1)}, u32[]{:S(2)}, u32[]{:S(2)}) %collective-permute-start.38) | collective-permute-done | bytes 884768 | tf_op jit(solution)/shard_map/ppermute | solution.py:289
  261.5 3.4 %collective-permute-done.40 = bf16[144,3072]{1,0:T(8,128)(2,1)S(1)} collective-permute-done((bf16[144,3072]{1,0:T(8,128)(2,1)S(1)}, bf16[144,3072]{1,0:T(8,128)(2,1)S(1)}, u32[]{:S(2)}, u32[]{:S(2)}) %collective-permute-start.40) | collective-permute-done | bytes 884768 | tf_op jit(solution)/shard_map/ppermute | solution.py:289
  264.9 1.3 add_convert_fusion.1
  266.2 1.6 collective-permute-start.42
  267.9 1.3 add_convert_fusion.4
  269.7 18.3 %collective-permute-done.42 = bf16[144,3072]{1,0:T(8,128)(2,1)S(1)} collective-permute-done((bf16[144,3072]{1,0:T(8,128)(2,1)}, bf16[144,3072]{1,0:T(8,128)(2,1)S(1)}, u32[]{:S(2)}, u32[]{:S(2)}) %collective-permute-start.42) | collective-permute-done | bytes 884768 | tf_op jit(solution)/shard_map/ppermute | solution.py:308
  288.9 1.8 collective-permute-done.41
  290.7 2.7 add_convert_fusion
  293.4 1.3 reshape.208
  294.7 3.6 %all-to-all-start.3 = ((bf16[8,18,3072]{2,1,0:T(8,128)(2,1)}), bf16[8,18,3072]{2,1,0:T(8,128)(2,1)S(1)}, u32[]{:S(2)}, u32[]{:S(2)}) async-start(bf16[8,18,3072]{2,1,0:T(8,128)(2,1)} %reshape.208), calls=%async_computation.3 | async-start | bytes 2359296 | tf_op jit(solution)/shard_map/all_to_all | solution.py:375
  298.3 2.5 collective-permute-start.12
  302.1 11.6 %all-to-all-done.3 = bf16[8,18,3072]{2,1,0:T(8,128)(2,1)S(1)} async-done(((bf16[8,18,3072]{2,1,0:T(8,128)(2,1)}), bf16[8,18,3072]{2,1,0:T(8,128)(2,1)S(1)}, u32[]{:S(2)}, u32[]{:S(2)}) %all-to-all-start.3) | async-done | bytes 884768 | tf_op jit(solution)/shard_map/all_to_all | solution.py:375
  314.5 2.7 collective-permute-start.43
  317.3 1.3 collective-permute-done.43
  (171 shorter events, 27.3 us)
Async XLA Ops:
  6.5 262.7 %copy-start = (f32[6144,8]{0,1:T(8,128)S(1)}, f32[6144,8]{0,1:T(8,128)}, u32[]{:S(2)}) copy-start(f32[6144,8]{0,1:T(8,128)} %param.20) | copy-start | bytes 589828
  6.5 64.9 %all-gather.2.cloned.1.call-start = ((), (), s32[]{:S(2)}) async-start(), calls=%async_computation.4 | async-start | bytes 2949120 | tf_op jit(solution)/shard_map/all_gather | solution.py:147
  9.6 13.2 %collective-permute-start = (bf16[272,128]{1,0:T(8,128)(2,1)S(1)}, bf16[272,128]{1,0:T(8,128)(2,1)S(1)}, u32[]{:S(2)}, u32[]{:S(2)}) collective-permute-start(bf16[272,128]{1,0:T(8,128)(2,1)S(1)} %pad_maximum_fusion.4), channel_id=1, source_target_pairs={{0,32},{16,48},{32,64},{48,80},{64,96},{80,112},{1,33},{17,49},{33... | collective-permute-start | bytes 208904 | tf_op jit(solution)/shard_map/ppermute | solution.py:32
  13.5 9.3 %collective-permute-start.1 = (bf16[272,128]{1,0:T(8,128)(2,1)S(1)}, bf16[272,128]{1,0:T(8,128)(2,1)S(1)}, u32[]{:S(2)}, u32[]{:S(2)}) collective-permute-start(bf16[272,128]{1,0:T(8,128)(2,1)S(1)} %pad_maximum_fusion.4), channel_id=1, source_target_pairs={{0,64},{16,80},{32,96},{48,112},{1,65},{17,81},{33,97},{49,113},{2... | collective-permute-start | bytes 208904 | tf_op jit(solution)/shard_map/ppermute | solution.py:32
  17.9 4.9 %collective-permute-start.2 = (bf16[272,128]{1,0:T(8,128)(2,1)S(1)}, bf16[272,128]{1,0:T(8,128)(2,1)S(1)}, u32[]{:S(2)}, u32[]{:S(2)}) collective-permute-start(bf16[272,128]{1,0:T(8,128)(2,1)S(1)} %pad_maximum_fusion.4), channel_id=1, source_target_pairs={{0,16},{16,0},{32,48},{48,32},{64,80},{80,64},{96,112},{112,96},{1... | collective-permute-start | bytes 208904 | tf_op jit(solution)/shard_map/ppermute | solution.py:32
  19.3 3.6 %collective-permute-start.3 = (bf16[272,128]{1,0:T(8,128)(2,1)S(1)}, bf16[272,128]{1,0:T(8,128)(2,1)S(1)}, u32[]{:S(2)}, u32[]{:S(2)}) collective-permute-start(bf16[272,128]{1,0:T(8,128)(2,1)S(1)} %pad_maximum_fusion.4), channel_id=1, source_target_pairs={{0,48},{16,32},{32,80},{48,64},{64,112},{80,96},{1,49},{17,33},{33... | collective-permute-start | bytes 208904 | tf_op jit(solution)/shard_map/ppermute | solution.py:32
  20.6 3.7 %collective-permute-start.4 = (bf16[272,128]{1,0:T(8,128)(2,1)S(1)}, bf16[272,128]{1,0:T(8,128)(2,1)S(1)}, u32[]{:S(2)}, u32[]{:S(2)}) collective-permute-start(bf16[272,128]{1,0:T(8,128)(2,1)S(1)} %pad_maximum_fusion.4), channel_id=1, source_target_pairs={{0,80},{16,64},{32,112},{48,96},{1,81},{17,65},{33,113},{49,97},{2... | collective-permute-start | bytes 208904 | tf_op jit(solution)/shard_map/ppermute | solution.py:32
  22.8 14.1 %copy-start.23 = (s32[4]{0:T(128)S(1)}, s32[4]{0:T(128)}, u32[]{:S(2)}) copy-start(s32[4]{0:T(128)} %constant.81.clone) | copy-start | bytes 52
  24.3 6.8 %collective-permute-start.9 = (bf16[192,768]{1,0:T(8,128)(2,1)}, bf16[192,768]{1,0:T(8,128)(2,1)S(1)}, u32[]{:S(2)}, u32[]{:S(2)}) collective-permute-start(bf16[192,768]{1,0:T(8,128)(2,1)} %bitcast.37), channel_id=1, source_target_pairs={{0,16},{16,0},{1,17},{17,1},{2,18},{18,2},{3,19},{19,3},{4,20},{20... | collective-permute-start | bytes 884744 | tf_op jit(solution)/shard_map/ppermute | solution.py:144
  25.1 24.8 %copy-start.1 = (bf16[128,768]{1,0:T(8,128)(2,1)S(1)}, bf16[128,768]{1,0:T(8,128)(2,1)}, u32[]{:S(2)}) copy-start(bf16[128,768]{1,0:T(8,128)(2,1)} %query.1) | copy-start | bytes 589828
  33.1 10.8 %collective-permute-start.5 = (bf16[1632,128]{1,0:T(8,128)(2,1)S(1)}, bf16[1632,128]{1,0:T(8,128)(2,1)S(1)}, u32[]{:S(2)}, u32[]{:S(2)}) collective-permute-start(bf16[1632,128]{1,0:T(8,128)(2,1)S(1)} %constant_dynamic-update-slice_fusion.here), channel_id=1, source_target_pairs={{0,4},{4,8},{8,12},{12,0},{1,5},{5,9},{9,13},{13,1},{2,6},{6,10},{... | collective-permute-start | bytes 1253384 | tf_op jit(solution)/shard_map/ppermute | solution.py:42
  34.7 9.3 %collective-permute-start.6 = (bf16[1632,128]{1,0:T(8,128)(2,1)S(1)}, bf16[1632,128]{1,0:T(8,128)(2,1)S(1)}, u32[]{:S(2)}, u32[]{:S(2)}) collective-permute-start(bf16[1632,128]{1,0:T(8,128)(2,1)S(1)} %constant_dynamic-update-slice_fusion.here), channel_id=1, source_target_pairs={{4,0},{8,4},{12,8},{0,12},{5,1},{9,5},{13,9},{1,13},{6,2},{10,6},{... | collective-permute-start | bytes 1253384 | tf_op jit(solution)/shard_map/ppermute | solution.py:43
  43.9 5.9 %collective-permute-start.7 = (bf16[816,128]{1,0:T(8,128)(2,1)S(1)}, bf16[816,128]{1,0:T(8,128)(2,1)S(1)}, u32[]{:S(2)}, u32[]{:S(2)}) collective-permute-start(bf16[816,128]{1,0:T(8,128)(2,1)S(1)} %slice.50), channel_id=1, source_target_pairs={{0,4},{4,8},{8,12},{12,0},{1,5},{5,9},{9,13},{13,1},{2,6},{6,10},{... | collective-permute-start | bytes 626696 | tf_op jit(solution)/shard_map/ppermute | solution.py:45
  44.1 5.8 %collective-permute-start.8 = (bf16[816,128]{1,0:T(8,128)(2,1)S(1)}, bf16[816,128]{1,0:T(8,128)(2,1)S(1)}, u32[]{:S(2)}, u32[]{:S(2)}) collective-permute-start(bf16[816,128]{1,0:T(8,128)(2,1)S(1)} %slice.51), channel_id=1, source_target_pairs={{4,0},{8,4},{12,8},{0,12},{5,1},{9,5},{13,9},{1,13},{6,2},{10,6},{... | collective-permute-start | bytes 626696 | tf_op jit(solution)/shard_map/ppermute | solution.py:46
  57.0 12.4 %all-to-all-start = ((bf16[4,128,768]{2,1,0:T(8,128)(2,1)}), bf16[4,128,768]{2,1,0:T(8,128)(2,1)S(1)}, u32[]{:S(2)}, u32[]{:S(2)}) async-start(bf16[4,128,768]{2,1,0:T(8,128)(2,1)} %broadcast_in_dim.66), calls=%async_computation | async-start | bytes 1572864 | tf_op jit(solution)/shard_map/all_to_all | solution.py:156
  74.6 6.3 %collective-permute-start.10 = (bf16[4,2,32,1536]{3,2,1,0:T(8,128)(2,1)S(1)}, bf16[4,2,32,1536]{3,2,1,0:T(8,128)(2,1)S(1)}, u32[]{:S(2)}, u32[]{:S(2)}) collective-permute-start(bf16[4,2,32,1536]{3,2,1,0:T(8,128)(2,1)S(1)} %dynamic-slice_bitcast_fusion), channel_id=1, source_target_pairs={{0,1},{1,0},{2,3},{3,2},{4,5},{5,4},{6,7},{7,6},{8,9},{9,8},{10,11... | collective-permute-start | bytes 2359304 | tf_op jit(solution)/shard_map/ppermute | solution.py:165
  79.0 7.5 %copy-start.16 = (s32[32,2]{0,1:T(2,128)S(1)}, s32[32,2]{0,1:T(2,128)}, u32[]{:S(2)}) copy-start(s32[32,2]{0,1:T(2,128)} %param.24) | copy-start | bytes 772
  82.0 18.0 %all-to-all-start.1 = ((bf16[8,32,1536]{2,1,0:T(8,128)(2,1)}), bf16[8,32,1536]{2,1,0:T(8,128)(2,1)S(1)}, u32[]{:S(2)}, u32[]{:S(2)}) async-start(bf16[8,32,1536]{2,1,0:T(8,128)(2,1)} %bitcast.10), calls=%async_computation.1 | async-start | bytes 1572864 | tf_op jit(solution)/shard_map/all_to_all | solution.py:167
  86.5 1.6 collective-permute-start.11
  101.0 1.7 copy-start.2
  103.1 3.0 copy-start.4
  103.2 3.0 collective-permute-start.13
  128.4 20.7 %collective-permute-start.14 = (bf16[144,3072]{1,0:T(8,128)(2,1)}, bf16[144,3072]{1,0:T(8,128)(2,1)S(1)}, u32[]{:S(2)}, u32[]{:S(2)}) collective-permute-start(bf16[144,3072]{1,0:T(8,128)(2,1)} %reshape.207.refs_0_), channel_id=1, source_target_pairs={{0,2},{2,0},{1,3},{3,1},{4,6},{6,4},{5,7},{7,5},{8,10},{10,8},{9,1... | collective-permute-start | bytes 2654216 | tf_op jit(solution)/shard_map/ppermute | solution.py:292
  129.9 22.3 %collective-permute-start.15 = (bf16[144,3072]{1,0:T(8,128)(2,1)}, bf16[144,3072]{1,0:T(8,128)(2,1)S(1)}, u32[]{:S(2)}, u32[]{:S(2)}) collective-permute-start(bf16[144,3072]{1,0:T(8,128)(2,1)} %reshape.207.refs_0_), channel_id=1, source_target_pairs={{0,4},{4,8},{8,12},{12,0},{1,5},{5,9},{9,13},{13,1},{2,6},{6,10},{... | collective-permute-start | bytes 2654216 | tf_op jit(solution)/shard_map/ppermute | solution.py:286
  130.4 23.2 %collective-permute-start.16 = (bf16[144,3072]{1,0:T(8,128)(2,1)}, bf16[144,3072]{1,0:T(8,128)(2,1)S(1)}, u32[]{:S(2)}, u32[]{:S(2)}) collective-permute-start(bf16[144,3072]{1,0:T(8,128)(2,1)} %reshape.207.refs_0_), channel_id=1, source_target_pairs={{4,0},{8,4},{12,8},{0,12},{5,1},{9,5},{13,9},{1,13},{6,2},{10,6},{... | collective-permute-start | bytes 2654216 | tf_op jit(solution)/shard_map/ppermute | solution.py:286
  132.8 21.8 %collective-permute-start.17 = (bf16[144,3072]{1,0:T(8,128)(2,1)}, bf16[144,3072]{1,0:T(8,128)(2,1)S(1)}, u32[]{:S(2)}, u32[]{:S(2)}) collective-permute-start(bf16[144,3072]{1,0:T(8,128)(2,1)} %reshape.207.refs_0_), channel_id=1, source_target_pairs={{0,1},{1,0},{2,3},{3,2},{4,5},{5,4},{6,7},{7,6},{8,9},{9,8},{10,11... | collective-permute-start | bytes 2654216 | tf_op jit(solution)/shard_map/ppermute | solution.py:278
  149.1 4.9 %copy-start.6 = (bf16[144,3072]{1,0:T(8,128)(2,1)}, bf16[144,3072]{1,0:T(8,128)(2,1)S(1)}, u32[]{:S(2)}) copy-start(bf16[144,3072]{1,0:T(8,128)(2,1)S(1)} %collective-permute-done.14.refs_1_) | copy-start | bytes 2654212
  149.1 7.8 %collective-permute-start.18 = (bf16[144,3072]{1,0:T(8,128)(2,1)S(1)}, bf16[144,3072]{1,0:T(8,128)(2,1)S(1)}, u32[]{:S(2)}, u32[]{:S(2)}) collective-permute-start(bf16[144,3072]{1,0:T(8,128)(2,1)S(1)} %collective-permute-done.14.refs_1_), channel_id=1, source_target_pairs={{0,1},{1,0},{2,3},{3,2},{4,5},{5,4},{6,7},{7,6},{8,9},{9,8},{10,11... | collective-permute-start | bytes 2654216 | tf_op jit(solution)/shard_map/ppermute | solution.py:278
  152.2 1.8 copy-start.14
  152.2 4.7 %collective-permute-start.19 = (bf16[144,3072]{1,0:T(8,128)(2,1)S(1)}, bf16[144,3072]{1,0:T(8,128)(2,1)S(1)}, u32[]{:S(2)}, u32[]{:S(2)}) collective-permute-start(bf16[144,3072]{1,0:T(8,128)(2,1)S(1)} %collective-permute-done.15.refs_2_), channel_id=1, source_target_pairs={{0,1},{1,0},{2,3},{3,2},{4,5},{5,4},{6,7},{7,6},{8,9},{9,8},{10,11... | collective-permute-start | bytes 2654216 | tf_op jit(solution)/shard_map/ppermute | solution.py:278
  153.6 3.3 %collective-permute-start.20 = (bf16[144,3072]{1,0:T(8,128)(2,1)S(1)}, bf16[144,3072]{1,0:T(8,128)(2,1)S(1)}, u32[]{:S(2)}, u32[]{:S(2)}) collective-permute-start(bf16[144,3072]{1,0:T(8,128)(2,1)S(1)} %collective-permute-done.16.refs_3_), channel_id=1, source_target_pairs={{0,1},{1,0},{2,3},{3,2},{4,5},{5,4},{6,7},{7,6},{8,9},{9,8},{10,11... | collective-permute-start | bytes 2654216 | tf_op jit(solution)/shard_map/ppermute | solution.py:278
  153.8 30.5 %collective-permute-start.26 = (bf16[208,3072]{1,0:T(8,128)(2,1)S(1)}, bf16[208,3072]{1,0:T(8,128)(2,1)S(1)}, u32[]{:S(2)}, u32[]{:S(2)}) collective-permute-start(bf16[208,3072]{1,0:T(8,128)(2,1)S(1)} %pad_maximum_fusion.1), channel_id=1, source_target_pairs={{0,4},{4,8},{8,12},{12,0},{1,5},{5,9},{9,13},{13,1},{2,6},{6,10},{... | collective-permute-start | bytes 3833864 | tf_op jit(solution)/shard_map/ppermute | solution.py:294
  154.6 4.1 %copy-start.18 = (bf16[144,3072]{1,0:T(8,128)(2,1)}, bf16[144,3072]{1,0:T(8,128)(2,1)S(1)}, u32[]{:S(2)}) copy-start(bf16[144,3072]{1,0:T(8,128)(2,1)S(1)} %collective-permute-done.17.refs_4_) | copy-start | bytes 2654212
  154.6 31.6 %collective-permute-start.27 = (bf16[224,3072]{1,0:T(8,128)(2,1)S(1)}, bf16[224,3072]{1,0:T(8,128)(2,1)S(1)}, u32[]{:S(2)}, u32[]{:S(2)}) collective-permute-start(bf16[224,3072]{1,0:T(8,128)(2,1)S(1)} %pad_maximum_fusion), channel_id=1, source_target_pairs={{4,0},{8,4},{12,8},{0,12},{5,1},{9,5},{13,9},{1,13},{6,2},{10,6},{... | collective-permute-start | bytes 4128776 | tf_op jit(solution)/shard_map/ppermute | solution.py:295
  156.8 1.9 copy-start.20
  177.9 9.6 %collective-permute-start.24 = (bf16[144,3072]{1,0:T(8,128)(2,1)S(1)}, bf16[144,3072]{1,0:T(8,128)(2,1)S(1)}, u32[]{:S(2)}, u32[]{:S(2)}) collective-permute-start(bf16[144,3072]{1,0:T(8,128)(2,1)S(1)} %get-tuple-element.31), channel_id=1, source_target_pairs={{0,1},{1,0},{2,3},{3,2},{4,5},{5,4},{6,7},{7,6},{8,9},{9,8},{10,11... | collective-permute-start | bytes 2654216 | tf_op jit(solution)/shard_map/ppermute | solution.py:283
  179.0 10.0 %collective-permute-start.22 = (bf16[144,3072]{1,0:T(8,128)(2,1)S(1)}, bf16[144,3072]{1,0:T(8,128)(2,1)S(1)}, u32[]{:S(2)}, u32[]{:S(2)}) collective-permute-start(bf16[144,3072]{1,0:T(8,128)(2,1)S(1)} %get-tuple-element.29), channel_id=1, source_target_pairs={{0,1},{1,0},{2,3},{3,2},{4,5},{5,4},{6,7},{7,6},{8,9},{9,8},{10,11... | collective-permute-start | bytes 2654216 | tf_op jit(solution)/shard_map/ppermute | solution.py:283
  179.1 10.2 %collective-permute-start.28 = (bf16[144,3072]{1,0:T(8,128)(2,1)S(1)}, bf16[144,3072]{1,0:T(8,128)(2,1)S(1)}, u32[]{:S(2)}, u32[]{:S(2)}) collective-permute-start(bf16[144,3072]{1,0:T(8,128)(2,1)S(1)} %get-tuple-element.33), channel_id=1, source_target_pairs={{0,1},{1,0},{2,3},{3,2},{4,5},{5,4},{6,7},{7,6},{8,9},{9,8},{10,11... | collective-permute-start | bytes 2654216 | tf_op jit(solution)/shard_map/ppermute | solution.py:283
  184.3 5.1 %collective-permute-start.21 = (bf16[144,3072]{1,0:T(8,128)(2,1)S(1)}, bf16[144,3072]{1,0:T(8,128)(2,1)S(1)}, u32[]{:S(2)}, u32[]{:S(2)}) collective-permute-start(bf16[144,3072]{1,0:T(8,128)(2,1)S(1)} %get-tuple-element.27), channel_id=1, source_target_pairs={{0,1},{1,0},{2,3},{3,2},{4,5},{5,4},{6,7},{7,6},{8,9},{9,8},{10,11... | collective-permute-start | bytes 2654216 | tf_op jit(solution)/shard_map/ppermute | solution.py:283
  185.7 1.8 copy-start.7
  186.2 6.5 %collective-permute-start.30 = (bf16[144,3072]{1,0:T(8,128)(2,1)S(1)}, bf16[144,3072]{1,0:T(8,128)(2,1)S(1)}, u32[]{:S(2)}, u32[]{:S(2)}) collective-permute-start(bf16[144,3072]{1,0:T(8,128)(2,1)S(1)} %slice.58.refs_1_), channel_id=1, source_target_pairs={{0,1},{1,0},{2,3},{3,2},{4,5},{5,4},{6,7},{7,6},{8,9},{9,8},{10,11... | collective-permute-start | bytes 2654216 | tf_op jit(solution)/shard_map/ppermute | solution.py:278
  187.4 1.4 copy-start.9
  187.5 1.7 copy-start.8
  187.5 17.1 %collective-permute-start.31 = (bf16[144,3072]{1,0:T(8,128)(2,1)S(1)}, bf16[144,3072]{1,0:T(8,128)(2,1)S(1)}, u32[]{:S(2)}, u32[]{:S(2)}) collective-permute-start(bf16[144,3072]{1,0:T(8,128)(2,1)S(1)} %slice.59.refs_2_), channel_id=1, source_target_pairs={{0,1},{1,0},{2,3},{3,2},{4,5},{5,4},{6,7},{7,6},{8,9},{9,8},{10,11... | collective-permute-start | bytes 2654216 | tf_op jit(solution)/shard_map/ppermute | solution.py:278
  189.7 14.9 %collective-permute-start.29 = (bf16[144,3072]{1,0:T(8,128)(2,1)S(1)}, bf16[144,3072]{1,0:T(8,128)(2,1)}, u32[]{:S(2)}, u32[]{:S(2)}) collective-permute-start(bf16[144,3072]{1,0:T(8,128)(2,1)S(1)} %pad_maximum_fusion.2.refs_0_), channel_id=1, source_target_pairs={{0,1},{1,0},{2,3},{3,2},{4,5},{5,4},{6,7},{7,6},{8,9},{9,8},{10,11... | collective-permute-start | bytes 2654216 | tf_op jit(solution)/shard_map/ppermute | solution.py:278
  189.8 31.4 %collective-permute-start.33 = (bf16[144,3072]{1,0:T(8,128)(2,1)S(1)}, bf16[144,3072]{1,0:T(8,128)(2,1)S(1)}, u32[]{:S(2)}, u32[]{:S(2)}) collective-permute-start(bf16[144,3072]{1,0:T(8,128)(2,1)S(1)} %pad_maximum_fusion.2.refs_0_), channel_id=1, source_target_pairs={{0,2},{2,0},{1,3},{3,1},{4,6},{6,4},{5,7},{7,5},{8,10},{10,8},{9,1... | collective-permute-start | bytes 2654216 | tf_op jit(solution)/shard_map/ppermute | solution.py:298
  191.3 29.9 %collective-permute-start.25 = (bf16[144,3072]{1,0:T(8,128)(2,1)S(1)}, bf16[144,3072]{1,0:T(8,128)(2,1)S(1)}, u32[]{:S(2)}, u32[]{:S(2)}) collective-permute-start(bf16[144,3072]{1,0:T(8,128)(2,1)S(1)} %add_convert_fusion.8), channel_id=1, source_target_pairs={{0,4},{4,8},{8,12},{12,0},{1,5},{5,9},{9,13},{13,1},{2,6},{6,10},{... | collective-permute-start | bytes 2654216 | tf_op jit(solution)/shard_map/ppermute | solution.py:289
  192.8 11.9 %copy-start.17 = (bf16[144,3072]{1,0:T(8,128)(2,1)}, bf16[144,3072]{1,0:T(8,128)(2,1)S(1)}, u32[]{:S(2)}) copy-start(bf16[144,3072]{1,0:T(8,128)(2,1)S(1)} %collective-permute-done.30.refs_4_) | copy-start | bytes 2654212
  192.8 30.2 %collective-permute-start.23 = (bf16[144,3072]{1,0:T(8,128)(2,1)S(1)}, bf16[144,3072]{1,0:T(8,128)(2,1)S(1)}, u32[]{:S(2)}, u32[]{:S(2)}) collective-permute-start(bf16[144,3072]{1,0:T(8,128)(2,1)S(1)} %add_convert_fusion.9), channel_id=1, source_target_pairs={{4,0},{8,4},{12,8},{0,12},{5,1},{9,5},{13,9},{1,13},{6,2},{10,6},{... | collective-permute-start | bytes 2654216 | tf_op jit(solution)/shard_map/ppermute | solution.py:289
  221.3 4.2 %copy-start.10 = (bf16[144,3072]{1,0:T(8,128)(2,1)}, bf16[144,3072]{1,0:T(8,128)(2,1)S(1)}, u32[]{:S(2)}) copy-start(bf16[144,3072]{1,0:T(8,128)(2,1)S(1)} %collective-permute-done.25) | copy-start | bytes 2654212
  223.9 3.6 %collective-permute-start.34 = (bf16[144,3072]{1,0:T(8,128)(2,1)S(1)}, bf16[144,3072]{1,0:T(8,128)(2,1)S(1)}, u32[]{:S(2)}, u32[]{:S(2)}) collective-permute-start(bf16[144,3072]{1,0:T(8,128)(2,1)S(1)} %collective-permute-done.33.refs_0_), channel_id=1, source_target_pairs={{0,1},{1,0},{2,3},{3,2},{4,5},{5,4},{6,7},{7,6},{8,9},{9,8},{10,11... | collective-permute-start | bytes 2654216 | tf_op jit(solution)/shard_map/ppermute | solution.py:278
  225.4 13.5 %collective-permute-start.37 = (bf16[144,3072]{1,0:T(8,128)(2,1)S(1)}, bf16[144,3072]{1,0:T(8,128)(2,1)S(1)}, u32[]{:S(2)}, u32[]{:S(2)}) collective-permute-start(bf16[144,3072]{1,0:T(8,128)(2,1)S(1)} %get-tuple-element.42), channel_id=1, source_target_pairs={{0,1},{1,0},{2,3},{3,2},{4,5},{5,4},{6,7},{7,6},{8,9},{9,8},{10,11... | collective-permute-start | bytes 2654216 | tf_op jit(solution)/shard_map/ppermute | solution.py:283
  225.4 17.2 %collective-permute-start.39 = (bf16[144,3072]{1,0:T(8,128)(2,1)S(1)}, bf16[144,3072]{1,0:T(8,128)(2,1)S(1)}, u32[]{:S(2)}, u32[]{:S(2)}) collective-permute-start(bf16[144,3072]{1,0:T(8,128)(2,1)S(1)} %get-tuple-element.43), channel_id=1, source_target_pairs={{0,1},{1,0},{2,3},{3,2},{4,5},{5,4},{6,7},{7,6},{8,9},{9,8},{10,11... | collective-permute-start | bytes 2654216 | tf_op jit(solution)/shard_map/ppermute | solution.py:283
  238.4 5.0 %collective-permute-start.35 = (bf16[144,3072]{1,0:T(8,128)(2,1)S(1)}, bf16[144,3072]{1,0:T(8,128)(2,1)S(1)}, u32[]{:S(2)}, u32[]{:S(2)}) collective-permute-start(bf16[144,3072]{1,0:T(8,128)(2,1)S(1)} %get-tuple-element.40), channel_id=1, source_target_pairs={{0,1},{1,0},{2,3},{3,2},{4,5},{5,4},{6,7},{7,6},{8,9},{9,8},{10,11... | collective-permute-start | bytes 2654216 | tf_op jit(solution)/shard_map/ppermute | solution.py:283
  239.1 22.4 %collective-permute-start.38 = (bf16[144,3072]{1,0:T(8,128)(2,1)S(1)}, bf16[144,3072]{1,0:T(8,128)(2,1)S(1)}, u32[]{:S(2)}, u32[]{:S(2)}) collective-permute-start(bf16[144,3072]{1,0:T(8,128)(2,1)S(1)} %add_convert_fusion.3), channel_id=1, source_target_pairs={{4,0},{8,4},{12,8},{0,12},{5,1},{9,5},{13,9},{1,13},{6,2},{10,6},{... | collective-permute-start | bytes 2654216 | tf_op jit(solution)/shard_map/ppermute | solution.py:289
  242.8 22.1 %collective-permute-start.40 = (bf16[144,3072]{1,0:T(8,128)(2,1)S(1)}, bf16[144,3072]{1,0:T(8,128)(2,1)S(1)}, u32[]{:S(2)}, u32[]{:S(2)}) collective-permute-start(bf16[144,3072]{1,0:T(8,128)(2,1)S(1)} %add_convert_fusion.2), channel_id=1, source_target_pairs={{0,4},{4,8},{8,12},{12,0},{1,5},{5,9},{9,13},{13,1},{2,6},{6,10},{... | collective-permute-start | bytes 2654216 | tf_op jit(solution)/shard_map/ppermute | solution.py:289
  242.9 24.9 %collective-permute-start.32 = (bf16[144,3072]{1,0:T(8,128)(2,1)S(1)}, bf16[144,3072]{1,0:T(8,128)(2,1)S(1)}, u32[]{:S(2)}, u32[]{:S(2)}) collective-permute-start(bf16[144,3072]{1,0:T(8,128)(2,1)S(1)} %get-tuple-element.36), channel_id=1, source_target_pairs={{0,1},{1,0},{2,3},{3,2},{4,5},{5,4},{6,7},{7,6},{8,9},{9,8},{10,11... | collective-permute-start | bytes 2654216 | tf_op jit(solution)/shard_map/ppermute | solution.py:283
  243.6 24.2 %collective-permute-start.36 = (bf16[144,3072]{1,0:T(8,128)(2,1)S(1)}, bf16[144,3072]{1,0:T(8,128)(2,1)S(1)}, u32[]{:S(2)}, u32[]{:S(2)}) collective-permute-start(bf16[144,3072]{1,0:T(8,128)(2,1)S(1)} %add_convert_fusion.5), channel_id=1, source_target_pairs={{0,2},{2,0},{1,3},{3,1},{4,6},{6,4},{5,7},{7,5},{8,10},{10,8},{9,1... | collective-permute-start | bytes 2654216 | tf_op jit(solution)/shard_map/ppermute | solution.py:307
  266.2 21.7 %collective-permute-start.42 = (bf16[144,3072]{1,0:T(8,128)(2,1)}, bf16[144,3072]{1,0:T(8,128)(2,1)S(1)}, u32[]{:S(2)}, u32[]{:S(2)}) collective-permute-start(bf16[144,3072]{1,0:T(8,128)(2,1)} %add_convert_fusion.1), channel_id=1, source_target_pairs={{0,2},{2,0},{1,3},{3,1},{4,6},{6,4},{5,7},{7,5},{8,10},{10,8},{9,1... | collective-permute-start | bytes 2654216 | tf_op jit(solution)/shard_map/ppermute | solution.py:308
  269.2 21.5 %collective-permute-start.41 = (bf16[144,3072]{1,0:T(8,128)(2,1)}, bf16[144,3072]{1,0:T(8,128)(2,1)}, u32[]{:S(2)}, u32[]{:S(2)}) collective-permute-start(bf16[144,3072]{1,0:T(8,128)(2,1)} %add_convert_fusion.4), channel_id=1, source_target_pairs={{0,8},{4,12},{8,0},{12,4},{1,9},{5,13},{9,1},{13,5},{2,10},{6,14},... | collective-permute-start | bytes 2654216 | tf_op jit(solution)/shard_map/ppermute | solution.py:309
  294.7 19.0 %all-to-all-start.3 = ((bf16[8,18,3072]{2,1,0:T(8,128)(2,1)}), bf16[8,18,3072]{2,1,0:T(8,128)(2,1)S(1)}, u32[]{:S(2)}, u32[]{:S(2)}) async-start(bf16[8,18,3072]{2,1,0:T(8,128)(2,1)} %reshape.208), calls=%async_computation.3 | async-start | bytes 2359296 | tf_op jit(solution)/shard_map/all_to_all | solution.py:375
  298.3 3.3 %collective-permute-start.12 = (f32[32,2]{0,1:T(2,128)S(1)}, f32[32,2]{0,1:T(2,128)S(1)}, u32[]{:S(2)}, u32[]{:S(2)}) collective-permute-start(f32[32,2]{0,1:T(2,128)S(1)} %pad_maximum_fusion.5), channel_id=1, source_target_pairs={{0,1},{1,0},{2,3},{3,2},{4,5},{5,4},{6,7},{7,6},{8,9},{9,8},{10,11... | collective-permute-start | bytes 776 | tf_op jit(solution)/shard_map/ppermute | solution.py:367
  313.9 4.7 %copy-start.3 = (bf16[32,6144]{1,0:T(8,128)(2,1)S(1)}, bf16[32,6144]{1,0:T(8,128)(2,1)}, u32[]{:S(2)}) copy-start(bf16[32,6144]{1,0:T(8,128)(2,1)} %param.13) | copy-start | bytes 1179652
  314.5 4.1 %collective-permute-start.43 = (f32[32,3072]{1,0:T(8,128)S(1)}, f32[32,3072]{1,0:T(8,128)S(1)}, u32[]{:S(2)}, u32[]{:S(2)}) collective-permute-start(f32[32,3072]{1,0:T(8,128)S(1)} %get-tuple-element.46), channel_id=1, source_target_pairs={{0,1},{1,0},{2,3},{3,2},{4,5},{5,4},{6,7},{7,6},{8,9},{9,8},{10,11... | collective-permute-start | bytes 1179656 | tf_op jit(solution)/shard_map/ppermute | solution.py:381
  (8 other events, 8.2 us)
Sparse Core Ops, SparseCore 0:
  33.1 38.3 all-gather.1
where the time goes:
time: 331 us; the launch traced here: 327 us
  waiting for transfers between devices  118 us (36%)
  starting transfers between devices  87.6 us (26%)
  Pallas kernels  51.9 us (16%)
  blocking collectives  20.3 us (6%)
  local copies, waits for them, and re-layouts  16 us (5%)
  other arithmetic  14.3 us (4%)
  between operations  14.3 us (4%)
  matrix products  4.43 us (1%)
    pallas_call x3, Pallas kernels, expert_part(): pl.pallas_call(functools.partial(expert_kernel, count), grid_spec=pltpu.P...  45.8 us
    ppermute x4, waiting for transfers between devices, near_back(): return (lax.ppermute(below, 'z', DOWN), lax.ppermute(above, 'z', UP))  21.4 us
    all_to_all x1, blocking collectives, per_device(): lax.all_to_all(packed.reshape(experts, cap, half), ('x', 'yl'), split_axi...  20.3 us
    ppermute x1, waiting for transfers between devices, experts_of(): over = lax.ppermute(add(over, *over_back), 'yh', SWAP)  18.3 us
    ppermute x4, starting transfers between devices, near_back(): return (lax.ppermute(below, 'z', DOWN), lax.ppermute(above, 'z', UP))  16.8 us
    ppermute x1, waiting for transfers between devices, experts_of(): over = lax.ppermute(own, 'yh', SWAP)  13.6 us
    ppermute x5, starting transfers between devices, from_behind(): return lax.ppermute(array, ('x', 'yl'), route)  13.1 us
    all_to_all x1, waiting for transfers between devices, per_device(): lax.all_to_all(home.reshape(experts, cap, half), ('x', 'yl'), split_axis=...  11.6 us
  transfers between devices with their start and end apart: 48, of which 23 were waited for; matrix products, arithmetic and copies ran while one was open for 3% of the time, Pallas kernels for 16%

commit v1 on v0

--- a/solution.py
+++ b/solution.py
@@ -12,6 +12,7 @@
 SWAP = [(0, 1), (1, 0)]
 UP = [(i, (i + 1) % NZ) for i in range(NZ)]
 DOWN = [((i + 1) % NZ, i) for i in range(NZ)]
+FAR = [(i, (i + 2) % NZ) for i in range(NZ)]
 
 
 def add(*terms):
@@ -25,10 +26,13 @@
     return lax.optimization_barrier((value, *others))[0]
 
 
-def from_behind(array, back, flip):
-    route = [
-        (x * NYL + yl, (x + back) * NYL + (yl ^ flip)) for x in range(NX - back) for yl in range(NYL)
-    ]
+def over_ctx(array, move):
+    route = []
+    for x in range(NX):
+        for yl in range(NYL):
+            to_x, to_yl = move(x, yl)
+            if to_x < NX:
+                route.append((x * NYL + yl, to_x * NYL + to_yl))
     return lax.ppermute(array, ("x", "yl"), route)
 
 
@@ -36,44 +40,68 @@
     tok = keys.shape[0]
     docs = jnp.pad(doc_ids.astype(jnp.bfloat16)[None, :], ((0, 15), (0, 0)))
     own = jnp.concatenate([keys, values, docs], axis=0)
-    order = [(flip, back) for flip in range(NYL) for back in range(3)]
-    pieces = [from_behind(own, back, flip) if flip or back else own for flip, back in order]
-    here = jnp.concatenate(pieces, axis=0)
-    below = lax.ppermute(here, "z", UP)
-    above = lax.ppermute(here, "z", DOWN)
-    half = here.shape[0] // 2
-    far_first = lax.ppermute(below[:half], "z", UP)
-    far_second = lax.ppermute(above[half:], "z", DOWN)
+    size = own.shape[0]
+    one = over_ctx(own, lambda x, yl: (x + 1, yl))
+    two = over_ctx(own, lambda x, yl: (x + 2, yl))
+    one_other = over_ctx(own, lambda x, yl: (x + 1, 1 - yl))
+    other = over_ctx(own, lambda x, yl: (x, 1) if yl == 0 else (x + 2, 0))
     x, yl, z = lax.axis_index("x"), lax.axis_index("yl"), lax.axis_index("z")
-    at_x = x - jnp.arange(3, dtype=jnp.int32)
-    at_yl = jnp.stack([yl, 1 - yl])
-    at_z = (z + jnp.array([0, 3, 1, 2], jnp.int32)) % NZ
-    base = (at_x[None, None, :] * NYL + at_yl[None, :, None]) * NZ + at_z[:, None, None]
-    base = jnp.where(at_x[None, None, :] >= 0, base * tok, 1 << 30).reshape(-1)
-    own_base = ((x * NYL + yl) * NZ + z) * tok
-    return (here, below, above, far_first, far_second), jnp.append(base, own_base)
-
-
-def attention_kernel(base, query, query_doc, here, below, above, far_a, far_b, out, *scratch):
+    up = jnp.concatenate([other, one_other, one, jnp.where(z == NZ - 1, two, own)], axis=0)
+    down = jnp.concatenate([other, one_other, one, jnp.where(z == 0, own, two)], axis=0)
+    below = lax.ppermute(up, "z", UP)
+    above = lax.ppermute(down, "z", DOWN)
+    far = lax.ppermute(jnp.where(z < 2, own, two), "z", FAR)
+    far_up = lax.ppermute(below[: 2 * size], "z", UP)
+    far_down = lax.ppermute(above[2 * size : 3 * size], "z", DOWN)
+
+    def base(at_x, at_yl, at_z):
+        return jnp.where(at_x >= 0, ((at_x * NYL + at_yl) * NZ + at_z) * tok, 1 << 30)
+
+    def column(at_z):
+        return [
+            base(jnp.where(yl == 1, x, x - 2), 1 - yl, at_z),
+            base(x - 1, 1 - yl, at_z),
+            base(x - 1, yl, at_z),
+            base(jnp.where(at_z < z, x, x - 2), yl, at_z),
+        ]
+
+    bases = [base(x, yl, z), base(x - 2, yl, z)] + column(z)[:3]
+    for step in (NZ - 1, 1, 2):
+        bases += column((z + step) % NZ)
+    return (own, two, up, below, above, far_up, far_down, far), jnp.stack(bases), (one, two, one_other, other)
+
+
+def attention_kernel(base, query, query_doc, own, two, mid, below, above, far_up, far_down, far, out, *scratch):
     rows, keys, vals, bias, scores, peak, total, accum = scratch
     tok = query.shape[0]
     heads = query.shape[1] // HEAD_WIDTH
     width = HEAD_WIDTH
-    step = here.shape[0] // 6
-    blocks = [(ref, i * step) for ref in (here, below, above) for i in range(6)]
-    blocks += [(ref, i * step) for ref in (far_a, far_b) for i in range(3)]
-    count = len(blocks)
-    wide = 4 * tok
+    step = own.shape[0]
+    blocks = []
+    for ref, count in (
+        (own, 1), (two, 1), (mid, 3), (below, 4), (above, 4), (far_up, 2), (far_down, 1), (far, 1)
+    ):
+        blocks += [(ref, i * step) for i in range(count)]
+    per = bias.shape[2] // tok
+    wide = per * tok
     for h in range(heads):
         rows[h * tok : (h + 1) * tok] = query[:, h * width : (h + 1) * width]
-    query_at = base[count] + lax.broadcasted_iota(jnp.int32, (tok, tok), 0)
+    query_at = base[0] + lax.broadcasted_iota(jnp.int32, (tok, tok), 0)
     lane = lax.broadcasted_iota(jnp.int32, (tok, tok), 1)
-    for i, (ref, first) in enumerate(blocks):
-        keys[i * tok : (i + 1) * tok] = ref[first : first + tok]
-        vals[i * tok : (i + 1) * tok] = ref[first + tok : first + 2 * tok]
-        docs = ref[first + 2 * tok : first + step].astype(jnp.float32)[0:1]
-        allowed = (docs == query_doc[...]) & (base[i] + lane <= query_at)
-        bias[i // 4, :, (i % 4) * tok : (i % 4 + 1) * tok] = jnp.where(allowed, 0.0, -1e30)
+    for i in range(per * bias.shape[0]):
+        at = pl.ds(i * tok, tok)
+        if i < len(blocks):
+            ref, first = blocks[i]
+            keys[at] = ref[first : first + tok]
+            vals[at] = ref[first + tok : first + 2 * tok]
+            docs = ref[first + 2 * tok : first + step].astype(jnp.float32)[0:1]
+            allowed = (docs == query_doc[...]) & (base[i] + lane <= query_at)
+            mask = jnp.where(allowed, 0.0, -1e30)
+        else:
+            keys[at] = jnp.zeros((tok, width), jnp.bfloat16)
+            vals[at] = jnp.zeros((tok, width), jnp.bfloat16)
+            mask = jnp.full((tok, tok), -1e30, jnp.float32)
+        bias[i // per, :, (i % per) * tok : (i % per + 1) * tok] = mask
     peak[...] = jnp.full(peak.shape, -1e30, jnp.float32)
     total[...] = jnp.zeros_like(total)
     accum[...] = jnp.zeros_like(accum)
@@ -81,7 +109,7 @@
     def lanes(array):
         return [array[:, i * width : (i + 1) * width] for i in range(wide // width)]
 
-    @pl.loop(0, count // 4)
+    @pl.loop(0, bias.shape[0])
     def _(i):
         at = pl.ds(pl.multiple_of(i * wide, wide), wide)
         value = lax.dot_general(
@@ -95,7 +123,7 @@
     top = jnp.max(peak[...], axis=1, keepdims=True)
     peak[...] = jnp.broadcast_to(top, peak.shape)
 
-    @pl.loop(0, count // 4)
+    @pl.loop(0, bias.shape[0])
     def _(i):
         at = pl.ds(pl.multiple_of(i * wide, wide), wide)
         expo = jnp.exp(scores[i] - jnp.concatenate([peak[...]] * (wide // width), axis=1))
@@ -112,36 +140,38 @@
 def attention(queries, keys, values, doc_ids):
     tok, columns = queries.shape
     heads = columns // HEAD_WIDTH
-    arrays, base = gather_keys(keys, values, doc_ids)
+    arrays, base, first = gather_keys(keys, values, doc_ids)
     whole = pl.BlockSpec(memory_space=pltpu.VMEM)
-    return pl.pallas_call(
+    turns, wide = 3, 6 * tok
+    out = pl.pallas_call(
         attention_kernel,
-        in_specs=[pl.BlockSpec(memory_space=pltpu.SMEM)] + [whole] * 7,
+        in_specs=[pl.BlockSpec(memory_space=pltpu.SMEM)] + [whole] * (2 + len(arrays)),
         out_specs=whole,
         out_shape=jax.ShapeDtypeStruct(queries.shape, jnp.bfloat16),
         scratch_shapes=[
             pltpu.VMEM((heads * tok, HEAD_WIDTH), jnp.bfloat16),
-            pltpu.VMEM((24 * tok, HEAD_WIDTH), jnp.bfloat16),
-            pltpu.VMEM((24 * tok, HEAD_WIDTH), jnp.bfloat16),
-            pltpu.VMEM((6, tok, 4 * tok), jnp.float32),
-            pltpu.VMEM((6, heads * tok, 4 * tok), jnp.float32),
+            pltpu.VMEM((turns * wide, HEAD_WIDTH), jnp.bfloat16),
+            pltpu.VMEM((turns * wide, HEAD_WIDTH), jnp.bfloat16),
+            pltpu.VMEM((turns, tok, wide), jnp.float32),
+            pltpu.VMEM((turns, heads * tok, wide), jnp.float32),
             pltpu.VMEM((heads * tok, HEAD_WIDTH), jnp.float32),
             pltpu.VMEM((heads * tok, HEAD_WIDTH), jnp.float32),
             pltpu.VMEM((heads * tok, HEAD_WIDTH), jnp.float32),
         ],
         compiler_params=pltpu.CompilerParams(vmem_limit_bytes=40 * 1024 * 1024),
         cost_estimate=pl.CostEstimate(
-            flops=4 * heads * tok * 24 * tok * HEAD_WIDTH,
-            bytes_accessed=4 * 24 * tok * HEAD_WIDTH,
-            transcendentals=heads * tok * 24 * tok,
+            flops=4 * heads * tok * turns * wide * HEAD_WIDTH,
+            bytes_accessed=4 * turns * wide * HEAD_WIDTH,
+            transcendentals=heads * tok * turns * wide,
         ),
         name="attention",
-    )(base, queries, doc_ids.astype(jnp.float32)[:, None], *arrays), arrays[0]
-
-
-def gather_projection(out_proj):
+    )(base, queries, doc_ids.astype(jnp.float32)[:, None], *arrays)
+    return out, first
+
+
+def gather_projection(out_proj, earlier):
     own = out_proj.T
-    other = lax.ppermute(own, "yl", SWAP)
+    other = after(lax.ppermute(own, "yl", SWAP), *earlier)
     first = lax.axis_index("yl") == 0
     pair = jnp.concatenate([jnp.where(first, own, other), jnp.where(first, other, own)], axis=0)
     return lax.all_gather(pair, "x", axis=0, tiled=True)
@@ -306,7 +336,7 @@
     (far_over,) = summed(last)
     far_own = add(far_own, lax.ppermute(far_over, "yh", SWAP))
     over = lax.ppermute(add(over, *over_back), "yh", SWAP)
-    far_own = lax.ppermute(after(far_own, *over_back), "z", [(i, (i + 2) % NZ) for i in range(NZ)])
+    far_own = lax.ppermute(after(far_own, *over_back), "z", FAR)
     return add(own, *own_back, far_own, over)
 
 
@@ -324,8 +354,8 @@
     w_down,
     routes,
 ):
-    heads_out, gathered = attention(queries, rotated_key_heads, values, doc_ids)
-    summed = project(heads_out, gather_projection(after(out_proj, gathered)))
+    heads_out, first_keys = attention(queries, rotated_key_heads, values, doc_ids)
+    summed = project(heads_out, gather_projection(out_proj, first_keys))
     resid = stream_in.astype(jnp.float32) + summed.astype(jnp.float32)
     width = resid.shape[1]
     normed = (

time: 331 us -> 317 us (0.958)
  waiting for transfers between devices: 118 us -> 112 us
    ppermute x11, waiting for transfers between devices: 18.8 us -> 10.8 us  [the longest x1 5.11 us: gather_keys(): below = lax.ppermute(up, 'z', UP)]
    unnamed x54 -> x50, local copies, waits for them, and re-layouts: 8.01 us -> 6.29 us
where the time goes in v1:
time: 317 us; the launch traced here: 312 us
  waiting for transfers between devices  112 us (35%)
  starting transfers between devices  84.3 us (27%)
  Pallas kernels  50.2 us (16%)
  blocking collectives  18.6 us (6%)
  between operations  14.3 us (5%)
  local copies, waits for them, and re-layouts  14.2 us (4%)
  other arithmetic  14.1 us (4%)
  matrix products  4.43 us (1%)
    pallas_call x3, Pallas kernels, expert_part(): pl.pallas_call(functools.partial(expert_kernel, count), grid_spec=pltpu.P...  45.8 us
    ppermute x4, waiting for transfers between devices, near_back(): return (lax.ppermute(below, 'z', DOWN), lax.ppermute(above, 'z', UP))  21.6 us
    all_to_all x1, blocking collectives, per_device(): lax.all_to_all(packed.reshape(experts, cap, half), ('x', 'yl'), split_axi...  18.6 us
    ppermute x1, waiting for transfers between devices, experts_of(): over = lax.ppermute(add(over, *over_back), 'yh', SWAP)  18.3 us
    ppermute x4, starting transfers between devices, near_back(): return (lax.ppermute(below, 'z', DOWN), lax.ppermute(above, 'z', UP))  16.8 us
    ppermute x1, waiting for transfers between devices, experts_of(): over = lax.ppermute(own, 'yh', SWAP)  14.2 us
    all_to_all x1, waiting for transfers between devices, per_device(): lax.all_to_all(home.reshape(experts, cap, half), ('x', 'yl'), split_axis=...  11.4 us
    ppermute x4, starting transfers between devices, over_ctx(): return lax.ppermute(array, ('x', 'yl'), route)  10.9 us
  transfers between devices with their start and end apart: 48, of which 23 were waited for; matrix products, arithmetic and copies ran while one was open for 3% of the time, Pallas kernels for 16%

profile of v1, /device:TPU:1, one launch (start us, length us, event | category | flops | bytes accessed | tf_op | source)
XLA Modules:
  0.0 312.4 jit_solution(3555015125320492114)
XLA Ops:
  6.5 2.2 collective-permute-start.9
  10.3 4.6 %collective-permute-start = (bf16[272,128]{1,0:T(8,128)(2,1)S(1)}, bf16[272,128]{1,0:T(8,128)(2,1)S(1)}, u32[]{:S(2)}, u32[]{:S(2)}) collective-permute-start(bf16[272,128]{1,0:T(8,128)(2,1)S(1)} %fusion.11.own), channel_id=1, source_target_pairs={{0,64},{16,80},{32,96},{48,112},{1,65},{17,81},{33,97},{49,113},{2... | collective-permute-start | bytes 208904 | tf_op jit(solution)/shard_map/ppermute | solution.py:36
  14.9 2.1 collective-permute-start.1
  17.0 2.3 collective-permute-start.2
  19.3 1.8 collective-permute-start.3
  21.2 1.9 collective-permute-done.3
  23.1 1.0 broadcast_select_fusion.1
  25.1 1.7 collective-permute-start.4
  26.8 2.2 collective-permute-start.5
  29.0 5.1 %collective-permute-done.4.below = bf16[1088,128]{1,0:T(8,128)(2,1)S(1)} collective-permute-done((bf16[1088,128]{1,0:T(8,128)(2,1)S(1)}, bf16[1088,128]{1,0:T(8,128)(2,1)S(1)}, u32[]{:S(2)}, u32[]{:S(2)}) %collective-permute-start.4) | collective-permute-done | bytes 278560 | tf_op jit(solution)/shard_map/ppermute | solution.py:51
  34.2 2.3 collective-permute-start.8
  37.6 2.2 collective-permute-done.8.far
  40.1 4.4 %attention.1 = bf16[128,768]{1,0:T(8,128)(2,1)S(1)} custom-call(s32[17]{0:T(128)S(1)} %stack.76.base, bf16[128,768]{1,0:T(8,128)(2,1)S(1)} %copy-done.1, f32[128,1]{1,0:T(8,128)S(1)} %copy.39.query_doc, bf16[272,128]{1,0:T(8,128)(2,1)S(1)} %fusion.11.own, bf16[272,128]{1,0:T(8,128)(2,1)S(1)} %collective-permute-done.two, ...), custom_call_target="tpu_custom_call" | custom-call | flops 905969664 | bytes 1179648 | tf_op jit(solution)/shard_map/attention/pallas_call | solution.py:146
  45.5 3.5 %all-to-all-start = ((bf16[4,128,768]{2,1,0:T(8,128)(2,1)}), bf16[4,128,768]{2,1,0:T(8,128)(2,1)S(1)}, u32[]{:S(2)}, u32[]{:S(2)}) async-start(bf16[4,128,768]{2,1,0:T(8,128)(2,1)} %broadcast_in_dim.48), calls=%async_computation | async-start | bytes 1572864 | tf_op jit(solution)/shard_map/all_to_all | solution.py:186
  49.0 8.4 %all-to-all-done = bf16[4,128,768]{2,1,0:T(8,128)(2,1)S(1)} async-done(((bf16[4,128,768]{2,1,0:T(8,128)(2,1)}), bf16[4,128,768]{2,1,0:T(8,128)(2,1)S(1)}, u32[]{:S(2)}, u32[]{:S(2)}) %all-to-all-start) | async-done | bytes 786464 | tf_op jit(solution)/shard_map/all_to_all | solution.py:186
  57.3 3.7 %all-gather.2.cloned.1.call-done = bf16[1536,768]{1,0:T(8,128)(2,1)} async-done(((bf16[384,768]{1,0:T(8,128)(2,1)}), bf16[1536,768]{1,0:T(8,128)(2,1)}) %all-gather.2.cloned.1.call-update) | async-done | bytes 2359312 | tf_op jit(solution)/shard_map/all_gather | solution.py:177
  61.0 3.1 convolution_convert_fusion.1
  64.2 1.6 collective-permute-start.10
  65.8 1.9 collective-permute-done.10
  67.7 1.1 fusion
  68.9 5.7 %all-to-all-start.1 = ((bf16[8,32,1536]{2,1,0:T(8,128)(2,1)}), bf16[8,32,1536]{2,1,0:T(8,128)(2,1)S(1)}, u32[]{:S(2)}, u32[]{:S(2)}) async-start(bf16[8,32,1536]{2,1,0:T(8,128)(2,1)} %bitcast.24), calls=%async_computation.1 | async-start | bytes 1572864 | tf_op jit(solution)/shard_map/all_to_all | solution.py:197
  77.3 10.8 %all-to-all-done.1 = bf16[8,32,1536]{2,1,0:T(8,128)(2,1)S(1)} async-done(((bf16[8,32,1536]{2,1,0:T(8,128)(2,1)}), bf16[8,32,1536]{2,1,0:T(8,128)(2,1)S(1)}, u32[]{:S(2)}, u32[]{:S(2)}) %all-to-all-start.1) | async-done | bytes 786464 | tf_op jit(solution)/shard_map/all_to_all | solution.py:197
  89.7 0.9 reshape.146
  91.2 1.9 collective-permute-start.13
  94.9 18.6 %all_to_all.20 = bf16[8,18,3072]{2,1,0:T(8,128)(2,1)S(1)} all-to-all(bf16[8,18,3072]{2,1,0:T(8,128)(2,1)S(1)} %reshape.148), channel_id=1, replica_groups=mesh['x'=4,'yl'=2,'z'=4,'yh'=2,'c'=2] {'x','yl'}, dimensions={0} | all-to-all | bytes 1769472 | tf_op jit(solution)/shard_map/all_to_all | solution.py:401
  113.5 1.2 reshape.149.refs_0_
  114.7 1.2 collective-permute-start.14
  116.4 2.4 collective-permute-start.16
  118.8 2.7 collective-permute-start.17
  121.5 14.2 %collective-permute-done.14.refs_1_ = bf16[144,3072]{1,0:T(8,128)(2,1)S(1)} collective-permute-done((bf16[144,3072]{1,0:T(8,128)(2,1)}, bf16[144,3072]{1,0:T(8,128)(2,1)S(1)}, u32[]{:S(2)}, u32[]{:S(2)}) %collective-permute-start.14) | collective-permute-done | bytes 884768 | tf_op jit(solution)/shard_map/ppermute | solution.py:322
  135.7 2.8 collective-permute-start.18
  138.5 1.1 collective-permute-start.19
  140.7 2.2 collective-permute-start.27
  143.8 1.0 copy-done.24
  144.8 19.2 %expert_part.3 = (bf16[144,3072]{1,0:T(8,128)(2,1)S(1)}, bf16[144,3072]{1,0:T(8,128)(2,1)S(1)}, bf16[144,3072]{1,0:T(8,128)(2,1)S(1)}, bf16[144,3072]{1,0:T(8,12...) custom-call(s32[1]{0:T(128)} %bitcast.29.core_ref, ...), custom_call_target="tpu_custom_call" | custom-call | flops 10871635968 | bytes 33030144 | tf_op jit(solution)/shard_map/expert_part/pallas_call | solution.py:272
  164.0 1.0 collective-permute-start.24
  165.5 4.8 %collective-permute-done.26 = bf16[208,3072]{1,0:T(8,128)(2,1)S(1)} collective-permute-done((bf16[208,3072]{1,0:T(8,128)(2,1)S(1)}, bf16[208,3072]{1,0:T(8,128)(2,1)S(1)}, u32[]{:S(2)}, u32[]{:S(2)}) %collective-permute-start.26) | collective-permute-done | bytes 1277984 | tf_op jit(solution)/shard_map/ppermute | solution.py:324
  170.3 1.3 collective-permute-start.21
  172.2 1.1 collective-permute-start.30
  173.6 1.1 copy-done.9
  175.8 1.9 collective-permute-start.33
  177.7 1.4 collective-permute-start.25
  179.1 11.9 %collective-permute-start.23 = (bf16[144,3072]{1,0:T(8,128)(2,1)S(1)}, bf16[144,3072]{1,0:T(8,128)(2,1)S(1)}, u32[]{:S(2)}, u32[]{:S(2)}) collective-permute-start(bf16[144,3072]{1,0:T(8,128)(2,1)S(1)} %add_convert_fusion.9), channel_id=1, source_target_pairs={{4,0},{8,4},{12,8},{0,12},{5,1},{9,5},{13,9},{1,13},{6,2},{10,6},{... | collective-permute-start | bytes 2654216 | tf_op jit(solution)/shard_map/ppermute | solution.py:319
  191.9 15.7 %expert_part.4 = (bf16[144,3072]{1,0:T(8,128)(2,1)S(1)}, bf16[144,3072]{1,0:T(8,128)(2,1)S(1)}, bf16[144,3072]{1,0:T(8,128)(2,1)S(1)}, bf16[144,3072]{1,0:T(8,12...) custom-call(s32[1]{0:T(128)} %bitcast.29.core_ref, ...), custom_call_target="tpu_custom_call" | custom-call | flops 8153726976 | bytes 29491200 | tf_op jit(solution)/shard_map/expert_part/pallas_call | solution.py:272
  207.6 1.6 collective-permute-done.23
  210.2 1.6 collective-permute-start.34
  212.3 1.5 collective-permute-done.34.refs_1_
  213.8 11.0 %expert_part.5 = (bf16[144,3072]{1,0:T(8,128)(2,1)S(1)}, bf16[144,3072]{1,0:T(8,128)(2,1)S(1)}) custom-call(s32[1]{0:T(128)} %bitcast.29.core_ref, bf16[144,3072]{1,0:T(8,128)(2,1)S(1)} %collective-permute-done.33.refs_0_, bf16[144,3072]{1,0:T(8,128)(2,1)S(1)} %collective-permute-done.34.refs_1_, bf16[6144,512]{1,0:T(8,128)(2,1)} %refs_2_.1, ...), custom_call_target="tpu_custom_call" | custom-call | flops 2717908992 | bytes 22413312 | tf_op jit(solution)/shard_map/expert_part/pallas_call | solution.py:272
  225.5 3.5 %collective-permute-start.38 = (bf16[144,3072]{1,0:T(8,128)(2,1)S(1)}, bf16[144,3072]{1,0:T(8,128)(2,1)S(1)}, u32[]{:S(2)}, u32[]{:S(2)}) collective-permute-start(bf16[144,3072]{1,0:T(8,128)(2,1)S(1)} %add_convert_fusion.3), channel_id=1, source_target_pairs={{4,0},{8,4},{12,8},{0,12},{5,1},{9,5},{13,9},{1,13},{6,2},{10,6},{... | collective-permute-start | bytes 2654216 | tf_op jit(solution)/shard_map/ppermute | solution.py:319
  230.0 1.3 collective-permute-start.36
  231.2 16.6 %collective-permute-done.38 = bf16[144,3072]{1,0:T(8,128)(2,1)S(1)} collective-permute-done((bf16[144,3072]{1,0:T(8,128)(2,1)S(1)}, bf16[144,3072]{1,0:T(8,128)(2,1)S(1)}, u32[]{:S(2)}, u32[]{:S(2)}) %collective-permute-start.38) | collective-permute-done | bytes 884768 | tf_op jit(solution)/shard_map/ppermute | solution.py:319
  247.8 3.4 %collective-permute-done.40 = bf16[144,3072]{1,0:T(8,128)(2,1)S(1)} collective-permute-done((bf16[144,3072]{1,0:T(8,128)(2,1)S(1)}, bf16[144,3072]{1,0:T(8,128)(2,1)S(1)}, u32[]{:S(2)}, u32[]{:S(2)}) %collective-permute-start.40) | collective-permute-done | bytes 884768 | tf_op jit(solution)/shard_map/ppermute | solution.py:319
  251.2 1.3 add_convert_fusion.1
  252.6 1.2 collective-permute-start.42
  253.8 1.4 add_convert_fusion.4
  255.9 18.3 %collective-permute-done.42 = bf16[144,3072]{1,0:T(8,128)(2,1)S(1)} collective-permute-done((bf16[144,3072]{1,0:T(8,128)(2,1)}, bf16[144,3072]{1,0:T(8,128)(2,1)S(1)}, u32[]{:S(2)}, u32[]{:S(2)}) %collective-permute-start.42) | collective-permute-done | bytes 884768 | tf_op jit(solution)/shard_map/ppermute | solution.py:338
  275.2 1.3 collective-permute-done.41
  276.5 2.7 add_convert_fusion
  279.2 1.3 reshape.150
  280.5 3.6 %all-to-all-start.3 = ((bf16[8,18,3072]{2,1,0:T(8,128)(2,1)}), bf16[8,18,3072]{2,1,0:T(8,128)(2,1)S(1)}, u32[]{:S(2)}, u32[]{:S(2)}) async-start(bf16[8,18,3072]{2,1,0:T(8,128)(2,1)} %reshape.150), calls=%async_computation.3 | async-start | bytes 2359296 | tf_op jit(solution)/shard_map/all_to_all | solution.py:405
  284.1 2.5 collective-permute-start.12
  288.0 11.4 %all-to-all-done.3 = bf16[8,18,3072]{2,1,0:T(8,128)(2,1)S(1)} async-done(((bf16[8,18,3072]{2,1,0:T(8,128)(2,1)}), bf16[8,18,3072]{2,1,0:T(8,128)(2,1)S(1)}, u32[]{:S(2)}, u32[]{:S(2)}) %all-to-all-start.3) | async-done | bytes 884768 | tf_op jit(solution)/shard_map/all_to_all | solution.py:405
  300.3 2.8 collective-permute-start.43
  303.1 1.3 collective-permute-done.43
  (160 shorter events, 25.1 us)
Async XLA Ops:
  6.5 248.9 %copy-start = (f32[6144,8]{0,1:T(8,128)S(1)}, f32[6144,8]{0,1:T(8,128)}, u32[]{:S(2)}) copy-start(f32[6144,8]{0,1:T(8,128)} %param.19) | copy-start | bytes 589828
  6.5 18.5 %copy-start.16 = (bf16[128,128]{1,0:T(8,128)(2,1)S(1)}, bf16[128,128]{1,0:T(8,128)(2,1)}, u32[]{:S(2)}) copy-start(bf16[128,128]{1,0:T(8,128)(2,1)} %param.14) | copy-start | bytes 98308
  6.5 18.5 %copy-start.15 = (bf16[128,128]{1,0:T(8,128)(2,1)S(1)}, bf16[128,128]{1,0:T(8,128)(2,1)}, u32[]{:S(2)}) copy-start(bf16[128,128]{1,0:T(8,128)(2,1)} %param.15) | copy-start | bytes 98308
  6.5 54.5 %all-gather.2.cloned.1.call-start = ((), (), s32[]{:S(2)}) async-start(), calls=%async_computation.4 | async-start | bytes 2949120 | tf_op jit(solution)/shard_map/all_gather | solution.py:177
  6.5 16.6 %collective-permute-start.9 = (bf16[192,768]{1,0:T(8,128)(2,1)}, bf16[192,768]{1,0:T(8,128)(2,1)S(1)}, u32[]{:S(2)}, u32[]{:S(2)}) collective-permute-start(bf16[192,768]{1,0:T(8,128)(2,1)} %bitcast.51), channel_id=1, source_target_pairs={{0,16},{16,0},{1,17},{17,1},{2,18},{18,2},{3,19},{19,3},{4,20},{20... | collective-permute-start | bytes 884744 | tf_op jit(solution)/shard_map/ppermute | solution.py:174
  10.3 10.9 %collective-permute-start = (bf16[272,128]{1,0:T(8,128)(2,1)S(1)}, bf16[272,128]{1,0:T(8,128)(2,1)S(1)}, u32[]{:S(2)}, u32[]{:S(2)}) collective-permute-start(bf16[272,128]{1,0:T(8,128)(2,1)S(1)} %fusion.11.own), channel_id=1, source_target_pairs={{0,64},{16,80},{32,96},{48,112},{1,65},{17,81},{33,97},{49,113},{2... | collective-permute-start | bytes 208904 | tf_op jit(solution)/shard_map/ppermute | solution.py:36
  14.9 6.3 %collective-permute-start.1 = (bf16[272,128]{1,0:T(8,128)(2,1)S(1)}, bf16[272,128]{1,0:T(8,128)(2,1)S(1)}, u32[]{:S(2)}, u32[]{:S(2)}) collective-permute-start(bf16[272,128]{1,0:T(8,128)(2,1)S(1)} %fusion.11.own), channel_id=1, source_target_pairs={{0,16},{16,64},{32,48},{48,96},{64,80},{96,112},{1,17},{17,65},{33... | collective-permute-start | bytes 208904 | tf_op jit(solution)/shard_map/ppermute | solution.py:36
  17.0 4.2 %collective-permute-start.2 = (bf16[272,128]{1,0:T(8,128)(2,1)S(1)}, bf16[272,128]{1,0:T(8,128)(2,1)S(1)}, u32[]{:S(2)}, u32[]{:S(2)}) collective-permute-start(bf16[272,128]{1,0:T(8,128)(2,1)S(1)} %fusion.11.own), channel_id=1, source_target_pairs={{0,48},{16,32},{32,80},{48,64},{64,112},{80,96},{1,49},{17,33},{33... | collective-permute-start | bytes 208904 | tf_op jit(solution)/shard_map/ppermute | solution.py:36
  19.3 3.8 %collective-permute-start.3 = (bf16[272,128]{1,0:T(8,128)(2,1)S(1)}, bf16[272,128]{1,0:T(8,128)(2,1)S(1)}, u32[]{:S(2)}, u32[]{:S(2)}) collective-permute-start(bf16[272,128]{1,0:T(8,128)(2,1)S(1)} %fusion.11.own), channel_id=1, source_target_pairs={{0,32},{16,48},{32,64},{48,80},{64,96},{80,112},{1,33},{17,49},{33... | collective-permute-start | bytes 208904 | tf_op jit(solution)/shard_map/ppermute | solution.py:36
  24.1 16.0 %copy-start.1 = (bf16[128,768]{1,0:T(8,128)(2,1)S(1)}, bf16[128,768]{1,0:T(8,128)(2,1)}, u32[]{:S(2)}) copy-start(bf16[128,768]{1,0:T(8,128)(2,1)} %query.1) | copy-start | bytes 589828
  25.1 9.0 %collective-permute-start.4 = (bf16[1088,128]{1,0:T(8,128)(2,1)S(1)}, bf16[1088,128]{1,0:T(8,128)(2,1)S(1)}, u32[]{:S(2)}, u32[]{:S(2)}) collective-permute-start(bf16[1088,128]{1,0:T(8,128)(2,1)S(1)} %get-tuple-element.52.mid), channel_id=1, source_target_pairs={{0,4},{4,8},{8,12},{12,0},{1,5},{5,9},{9,13},{13,1},{2,6},{6,10},{... | collective-permute-start | bytes 835592 | tf_op jit(solution)/shard_map/ppermute | solution.py:51
  26.8 9.8 %collective-permute-start.5 = (bf16[1088,128]{1,0:T(8,128)(2,1)S(1)}, bf16[1088,128]{1,0:T(8,128)(2,1)S(1)}, u32[]{:S(2)}, u32[]{:S(2)}) collective-permute-start(bf16[1088,128]{1,0:T(8,128)(2,1)S(1)} %get-tuple-element.51), channel_id=1, source_target_pairs={{4,0},{8,4},{12,8},{0,12},{5,1},{9,5},{13,9},{1,13},{6,2},{10,6},{... | collective-permute-start | bytes 835592 | tf_op jit(solution)/shard_map/ppermute | solution.py:52
  34.2 5.9 %collective-permute-start.6 = (bf16[544,128]{1,0:T(8,128)(2,1)S(1)}, bf16[544,128]{1,0:T(8,128)(2,1)S(1)}, u32[]{:S(2)}, u32[]{:S(2)}) collective-permute-start(bf16[544,128]{1,0:T(8,128)(2,1)S(1)} %slice.50), channel_id=1, source_target_pairs={{0,4},{4,8},{8,12},{12,0},{1,5},{5,9},{9,13},{13,1},{2,6},{6,10},{... | collective-permute-start | bytes 417800 | tf_op jit(solution)/shard_map/ppermute | solution.py:54
  34.2 5.6 %collective-permute-start.8 = (bf16[272,128]{1,0:T(8,128)(2,1)S(1)}, bf16[272,128]{1,0:T(8,128)(2,1)S(1)}, u32[]{:S(2)}, u32[]{:S(2)}) collective-permute-start(bf16[272,128]{1,0:T(8,128)(2,1)S(1)} %get-tuple-element.53), channel_id=1, source_target_pairs={{0,8},{4,12},{8,0},{12,4},{1,9},{5,13},{9,1},{13,5},{2,10},{6,14},... | collective-permute-start | bytes 208904 | tf_op jit(solution)/shard_map/ppermute | solution.py:53
  36.6 3.3 %collective-permute-start.7 = (bf16[272,128]{1,0:T(8,128)(2,1)S(1)}, bf16[272,128]{1,0:T(8,128)(2,1)S(1)}, u32[]{:S(2)}, u32[]{:S(2)}) collective-permute-start(bf16[272,128]{1,0:T(8,128)(2,1)S(1)} %slice.51), channel_id=1, source_target_pairs={{4,0},{8,4},{12,8},{0,12},{5,1},{9,5},{13,9},{1,13},{6,2},{10,6},{... | collective-permute-start | bytes 208904 | tf_op jit(solution)/shard_map/ppermute | solution.py:55
  45.5 11.9 %all-to-all-start = ((bf16[4,128,768]{2,1,0:T(8,128)(2,1)}), bf16[4,128,768]{2,1,0:T(8,128)(2,1)S(1)}, u32[]{:S(2)}, u32[]{:S(2)}) async-start(bf16[4,128,768]{2,1,0:T(8,128)(2,1)} %broadcast_in_dim.48), calls=%async_computation | async-start | bytes 1572864 | tf_op jit(solution)/shard_map/all_to_all | solution.py:186
  64.2 3.6 %collective-permute-start.10 = (bf16[4,2,32,1536]{3,2,1,0:T(8,128)(2,1)S(1)}, bf16[4,2,32,1536]{3,2,1,0:T(8,128)(2,1)S(1)}, u32[]{:S(2)}, u32[]{:S(2)}) collective-permute-start(bf16[4,2,32,1536]{3,2,1,0:T(8,128)(2,1)S(1)} %dynamic-slice_bitcast_fusion), channel_id=1, source_target_pairs={{0,1},{1,0},{2,3},{3,2},{4,5},{5,4},{6,7},{7,6},{8,9},{9,8},{10,11... | collective-permute-start | bytes 2359304 | tf_op jit(solution)/shard_map/ppermute | solution.py:195
  65.8 8.7 %copy-start.18 = (s32[32,2]{0,1:T(2,128)S(1)}, s32[32,2]{0,1:T(2,128)}, u32[]{:S(2)}) copy-start(s32[32,2]{0,1:T(2,128)} %param.23) | copy-start | bytes 772
  68.9 19.2 %all-to-all-start.1 = ((bf16[8,32,1536]{2,1,0:T(8,128)(2,1)}), bf16[8,32,1536]{2,1,0:T(8,128)(2,1)S(1)}, u32[]{:S(2)}, u32[]{:S(2)}) async-start(bf16[8,32,1536]{2,1,0:T(8,128)(2,1)} %bitcast.24), calls=%async_computation.1 | async-start | bytes 1572864 | tf_op jit(solution)/shard_map/all_to_all | solution.py:197
  74.6 1.6 collective-permute-start.11
  89.0 1.7 copy-start.2
  91.1 3.0 copy-start.4
  91.2 3.0 collective-permute-start.13
  114.7 21.0 %collective-permute-start.14 = (bf16[144,3072]{1,0:T(8,128)(2,1)}, bf16[144,3072]{1,0:T(8,128)(2,1)S(1)}, u32[]{:S(2)}, u32[]{:S(2)}) collective-permute-start(bf16[144,3072]{1,0:T(8,128)(2,1)} %reshape.149.refs_0_), channel_id=1, source_target_pairs={{0,2},{2,0},{1,3},{3,1},{4,6},{6,4},{5,7},{7,5},{8,10},{10,8},{9,1... | collective-permute-start | bytes 2654216 | tf_op jit(solution)/shard_map/ppermute | solution.py:322
  115.9 22.6 %collective-permute-start.15 = (bf16[144,3072]{1,0:T(8,128)(2,1)}, bf16[144,3072]{1,0:T(8,128)(2,1)S(1)}, u32[]{:S(2)}, u32[]{:S(2)}) collective-permute-start(bf16[144,3072]{1,0:T(8,128)(2,1)} %reshape.149.refs_0_), channel_id=1, source_target_pairs={{0,4},{4,8},{8,12},{12,0},{1,5},{5,9},{9,13},{13,1},{2,6},{6,10},{... | collective-permute-start | bytes 2654216 | tf_op jit(solution)/shard_map/ppermute | solution.py:316
  116.4 23.2 %collective-permute-start.16 = (bf16[144,3072]{1,0:T(8,128)(2,1)}, bf16[144,3072]{1,0:T(8,128)(2,1)S(1)}, u32[]{:S(2)}, u32[]{:S(2)}) collective-permute-start(bf16[144,3072]{1,0:T(8,128)(2,1)} %reshape.149.refs_0_), channel_id=1, source_target_pairs={{4,0},{8,4},{12,8},{0,12},{5,1},{9,5},{13,9},{1,13},{6,2},{10,6},{... | collective-permute-start | bytes 2654216 | tf_op jit(solution)/shard_map/ppermute | solution.py:316
  118.8 21.9 %collective-permute-start.17 = (bf16[144,3072]{1,0:T(8,128)(2,1)}, bf16[144,3072]{1,0:T(8,128)(2,1)S(1)}, u32[]{:S(2)}, u32[]{:S(2)}) collective-permute-start(bf16[144,3072]{1,0:T(8,128)(2,1)} %reshape.149.refs_0_), channel_id=1, source_target_pairs={{0,1},{1,0},{2,3},{3,2},{4,5},{5,4},{6,7},{7,6},{8,9},{9,8},{10,11... | collective-permute-start | bytes 2654216 | tf_op jit(solution)/shard_map/ppermute | solution.py:308
  135.7 4.3 %copy-start.6 = (bf16[144,3072]{1,0:T(8,128)(2,1)}, bf16[144,3072]{1,0:T(8,128)(2,1)S(1)}, u32[]{:S(2)}) copy-start(bf16[144,3072]{1,0:T(8,128)(2,1)S(1)} %collective-permute-done.14.refs_1_) | copy-start | bytes 2654212
  135.7 7.1 %collective-permute-start.18 = (bf16[144,3072]{1,0:T(8,128)(2,1)S(1)}, bf16[144,3072]{1,0:T(8,128)(2,1)S(1)}, u32[]{:S(2)}, u32[]{:S(2)}) collective-permute-start(bf16[144,3072]{1,0:T(8,128)(2,1)S(1)} %collective-permute-done.14.refs_1_), channel_id=1, source_target_pairs={{0,1},{1,0},{2,3},{3,2},{4,5},{5,4},{6,7},{7,6},{8,9},{9,8},{10,11... | collective-permute-start | bytes 2654216 | tf_op jit(solution)/shard_map/ppermute | solution.py:308
  138.5 4.4 %collective-permute-start.19 = (bf16[144,3072]{1,0:T(8,128)(2,1)S(1)}, bf16[144,3072]{1,0:T(8,128)(2,1)S(1)}, u32[]{:S(2)}, u32[]{:S(2)}) collective-permute-start(bf16[144,3072]{1,0:T(8,128)(2,1)S(1)} %collective-permute-done.15.refs_2_), channel_id=1, source_target_pairs={{0,1},{1,0},{2,3},{3,2},{4,5},{5,4},{6,7},{7,6},{8,9},{9,8},{10,11... | collective-permute-start | bytes 2654216 | tf_op jit(solution)/shard_map/ppermute | solution.py:308
  139.6 3.4 %collective-permute-start.20 = (bf16[144,3072]{1,0:T(8,128)(2,1)S(1)}, bf16[144,3072]{1,0:T(8,128)(2,1)S(1)}, u32[]{:S(2)}, u32[]{:S(2)}) collective-permute-start(bf16[144,3072]{1,0:T(8,128)(2,1)S(1)} %collective-permute-done.16.refs_3_), channel_id=1, source_target_pairs={{0,1},{1,0},{2,3},{3,2},{4,5},{5,4},{6,7},{7,6},{8,9},{9,8},{10,11... | collective-permute-start | bytes 2654216 | tf_op jit(solution)/shard_map/ppermute | solution.py:308
  139.8 30.5 %collective-permute-start.26 = (bf16[208,3072]{1,0:T(8,128)(2,1)S(1)}, bf16[208,3072]{1,0:T(8,128)(2,1)S(1)}, u32[]{:S(2)}, u32[]{:S(2)}) collective-permute-start(bf16[208,3072]{1,0:T(8,128)(2,1)S(1)} %pad_maximum_fusion.1), channel_id=1, source_target_pairs={{0,4},{4,8},{8,12},{12,0},{1,5},{5,9},{9,13},{13,1},{2,6},{6,10},{... | collective-permute-start | bytes 3833864 | tf_op jit(solution)/shard_map/ppermute | solution.py:324
  140.7 4.1 %copy-start.20 = (bf16[144,3072]{1,0:T(8,128)(2,1)}, bf16[144,3072]{1,0:T(8,128)(2,1)S(1)}, u32[]{:S(2)}) copy-start(bf16[144,3072]{1,0:T(8,128)(2,1)S(1)} %collective-permute-done.17.refs_4_) | copy-start | bytes 2654212
  140.7 31.6 %collective-permute-start.27 = (bf16[224,3072]{1,0:T(8,128)(2,1)S(1)}, bf16[224,3072]{1,0:T(8,128)(2,1)S(1)}, u32[]{:S(2)}, u32[]{:S(2)}) collective-permute-start(bf16[224,3072]{1,0:T(8,128)(2,1)S(1)} %pad_maximum_fusion), channel_id=1, source_target_pairs={{4,0},{8,4},{12,8},{0,12},{5,1},{9,5},{13,9},{1,13},{6,2},{10,6},{... | collective-permute-start | bytes 4128776 | tf_op jit(solution)/shard_map/ppermute | solution.py:325
  142.8 1.9 copy-start.22
  164.0 9.6 %collective-permute-start.24 = (bf16[144,3072]{1,0:T(8,128)(2,1)S(1)}, bf16[144,3072]{1,0:T(8,128)(2,1)S(1)}, u32[]{:S(2)}, u32[]{:S(2)}) collective-permute-start(bf16[144,3072]{1,0:T(8,128)(2,1)S(1)} %get-tuple-element.31), channel_id=1, source_target_pairs={{0,1},{1,0},{2,3},{3,2},{4,5},{5,4},{6,7},{7,6},{8,9},{9,8},{10,11... | collective-permute-start | bytes 2654216 | tf_op jit(solution)/shard_map/ppermute | solution.py:313
  165.0 10.0 %collective-permute-start.22 = (bf16[144,3072]{1,0:T(8,128)(2,1)S(1)}, bf16[144,3072]{1,0:T(8,128)(2,1)S(1)}, u32[]{:S(2)}, u32[]{:S(2)}) collective-permute-start(bf16[144,3072]{1,0:T(8,128)(2,1)S(1)} %get-tuple-element.29), channel_id=1, source_target_pairs={{0,1},{1,0},{2,3},{3,2},{4,5},{5,4},{6,7},{7,6},{8,9},{9,8},{10,11... | collective-permute-start | bytes 2654216 | tf_op jit(solution)/shard_map/ppermute | solution.py:313
  165.1 10.2 %collective-permute-start.28 = (bf16[144,3072]{1,0:T(8,128)(2,1)S(1)}, bf16[144,3072]{1,0:T(8,128)(2,1)S(1)}, u32[]{:S(2)}, u32[]{:S(2)}) collective-permute-start(bf16[144,3072]{1,0:T(8,128)(2,1)S(1)} %get-tuple-element.33), channel_id=1, source_target_pairs={{0,1},{1,0},{2,3},{3,2},{4,5},{5,4},{6,7},{7,6},{8,9},{9,8},{10,11... | collective-permute-start | bytes 2654216 | tf_op jit(solution)/shard_map/ppermute | solution.py:313
  170.3 5.2 %collective-permute-start.21 = (bf16[144,3072]{1,0:T(8,128)(2,1)S(1)}, bf16[144,3072]{1,0:T(8,128)(2,1)S(1)}, u32[]{:S(2)}, u32[]{:S(2)}) collective-permute-start(bf16[144,3072]{1,0:T(8,128)(2,1)S(1)} %get-tuple-element.27), channel_id=1, source_target_pairs={{0,1},{1,0},{2,3},{3,2},{4,5},{5,4},{6,7},{7,6},{8,9},{9,8},{10,11... | collective-permute-start | bytes 2654216 | tf_op jit(solution)/shard_map/ppermute | solution.py:313
  171.7 1.8 copy-start.7
  172.2 6.8 %collective-permute-start.30 = (bf16[144,3072]{1,0:T(8,128)(2,1)S(1)}, bf16[144,3072]{1,0:T(8,128)(2,1)S(1)}, u32[]{:S(2)}, u32[]{:S(2)}) collective-permute-start(bf16[144,3072]{1,0:T(8,128)(2,1)S(1)} %slice.58.refs_1_), channel_id=1, source_target_pairs={{0,1},{1,0},{2,3},{3,2},{4,5},{5,4},{6,7},{7,6},{8,9},{9,8},{10,11... | collective-permute-start | bytes 2654216 | tf_op jit(solution)/shard_map/ppermute | solution.py:308
  173.5 1.7 copy-start.8
  173.6 17.4 %collective-permute-start.31 = (bf16[144,3072]{1,0:T(8,128)(2,1)S(1)}, bf16[144,3072]{1,0:T(8,128)(2,1)S(1)}, u32[]{:S(2)}, u32[]{:S(2)}) collective-permute-start(bf16[144,3072]{1,0:T(8,128)(2,1)S(1)} %slice.59.refs_2_), channel_id=1, source_target_pairs={{0,1},{1,0},{2,3},{3,2},{4,5},{5,4},{6,7},{7,6},{8,9},{9,8},{10,11... | collective-permute-start | bytes 2654216 | tf_op jit(solution)/shard_map/ppermute | solution.py:308
  175.7 15.2 %collective-permute-start.29 = (bf16[144,3072]{1,0:T(8,128)(2,1)S(1)}, bf16[144,3072]{1,0:T(8,128)(2,1)}, u32[]{:S(2)}, u32[]{:S(2)}) collective-permute-start(bf16[144,3072]{1,0:T(8,128)(2,1)S(1)} %pad_maximum_fusion.2.refs_0_), channel_id=1, source_target_pairs={{0,1},{1,0},{2,3},{3,2},{4,5},{5,4},{6,7},{7,6},{8,9},{9,8},{10,11... | collective-permute-start | bytes 2654216 | tf_op jit(solution)/shard_map/ppermute | solution.py:308
  175.8 31.7 %collective-permute-start.33 = (bf16[144,3072]{1,0:T(8,128)(2,1)S(1)}, bf16[144,3072]{1,0:T(8,128)(2,1)S(1)}, u32[]{:S(2)}, u32[]{:S(2)}) collective-permute-start(bf16[144,3072]{1,0:T(8,128)(2,1)S(1)} %pad_maximum_fusion.2.refs_0_), channel_id=1, source_target_pairs={{0,2},{2,0},{1,3},{3,1},{4,6},{6,4},{5,7},{7,5},{8,10},{10,8},{9,1... | collective-permute-start | bytes 2654216 | tf_op jit(solution)/shard_map/ppermute | solution.py:328
  177.7 29.9 %collective-permute-start.25 = (bf16[144,3072]{1,0:T(8,128)(2,1)S(1)}, bf16[144,3072]{1,0:T(8,128)(2,1)S(1)}, u32[]{:S(2)}, u32[]{:S(2)}) collective-permute-start(bf16[144,3072]{1,0:T(8,128)(2,1)S(1)} %add_convert_fusion.8), channel_id=1, source_target_pairs={{0,4},{4,8},{8,12},{12,0},{1,5},{5,9},{9,13},{13,1},{2,6},{6,10},{... | collective-permute-start | bytes 2654216 | tf_op jit(solution)/shard_map/ppermute | solution.py:319
  179.1 11.9 %copy-start.19 = (bf16[144,3072]{1,0:T(8,128)(2,1)}, bf16[144,3072]{1,0:T(8,128)(2,1)S(1)}, u32[]{:S(2)}) copy-start(bf16[144,3072]{1,0:T(8,128)(2,1)S(1)} %collective-permute-done.30.refs_4_) | copy-start | bytes 2654212
  179.1 30.2 %collective-permute-start.23 = (bf16[144,3072]{1,0:T(8,128)(2,1)S(1)}, bf16[144,3072]{1,0:T(8,128)(2,1)S(1)}, u32[]{:S(2)}, u32[]{:S(2)}) collective-permute-start(bf16[144,3072]{1,0:T(8,128)(2,1)S(1)} %add_convert_fusion.9), channel_id=1, source_target_pairs={{4,0},{8,4},{12,8},{0,12},{5,1},{9,5},{13,9},{1,13},{6,2},{10,6},{... | collective-permute-start | bytes 2654216 | tf_op jit(solution)/shard_map/ppermute | solution.py:319
  207.6 4.2 %copy-start.10 = (bf16[144,3072]{1,0:T(8,128)(2,1)}, bf16[144,3072]{1,0:T(8,128)(2,1)S(1)}, u32[]{:S(2)}) copy-start(bf16[144,3072]{1,0:T(8,128)(2,1)S(1)} %collective-permute-done.25) | copy-start | bytes 2654212
  210.2 3.6 %collective-permute-start.34 = (bf16[144,3072]{1,0:T(8,128)(2,1)S(1)}, bf16[144,3072]{1,0:T(8,128)(2,1)S(1)}, u32[]{:S(2)}, u32[]{:S(2)}) collective-permute-start(bf16[144,3072]{1,0:T(8,128)(2,1)S(1)} %collective-permute-done.33.refs_0_), channel_id=1, source_target_pairs={{0,1},{1,0},{2,3},{3,2},{4,5},{5,4},{6,7},{7,6},{8,9},{9,8},{10,11... | collective-permute-start | bytes 2654216 | tf_op jit(solution)/shard_map/ppermute | solution.py:308
  211.7 13.5 %collective-permute-start.37 = (bf16[144,3072]{1,0:T(8,128)(2,1)S(1)}, bf16[144,3072]{1,0:T(8,128)(2,1)S(1)}, u32[]{:S(2)}, u32[]{:S(2)}) collective-permute-start(bf16[144,3072]{1,0:T(8,128)(2,1)S(1)} %get-tuple-element.42), channel_id=1, source_target_pairs={{0,1},{1,0},{2,3},{3,2},{4,5},{5,4},{6,7},{7,6},{8,9},{9,8},{10,11... | collective-permute-start | bytes 2654216 | tf_op jit(solution)/shard_map/ppermute | solution.py:313
  211.7 17.2 %collective-permute-start.39 = (bf16[144,3072]{1,0:T(8,128)(2,1)S(1)}, bf16[144,3072]{1,0:T(8,128)(2,1)S(1)}, u32[]{:S(2)}, u32[]{:S(2)}) collective-permute-start(bf16[144,3072]{1,0:T(8,128)(2,1)S(1)} %get-tuple-element.43), channel_id=1, source_target_pairs={{0,1},{1,0},{2,3},{3,2},{4,5},{5,4},{6,7},{7,6},{8,9},{9,8},{10,11... | collective-permute-start | bytes 2654216 | tf_op jit(solution)/shard_map/ppermute | solution.py:313
  224.8 5.0 %collective-permute-start.35 = (bf16[144,3072]{1,0:T(8,128)(2,1)S(1)}, bf16[144,3072]{1,0:T(8,128)(2,1)S(1)}, u32[]{:S(2)}, u32[]{:S(2)}) collective-permute-start(bf16[144,3072]{1,0:T(8,128)(2,1)S(1)} %get-tuple-element.40), channel_id=1, source_target_pairs={{0,1},{1,0},{2,3},{3,2},{4,5},{5,4},{6,7},{7,6},{8,9},{9,8},{10,11... | collective-permute-start | bytes 2654216 | tf_op jit(solution)/shard_map/ppermute | solution.py:313
  225.5 22.4 %collective-permute-start.38 = (bf16[144,3072]{1,0:T(8,128)(2,1)S(1)}, bf16[144,3072]{1,0:T(8,128)(2,1)S(1)}, u32[]{:S(2)}, u32[]{:S(2)}) collective-permute-start(bf16[144,3072]{1,0:T(8,128)(2,1)S(1)} %add_convert_fusion.3), channel_id=1, source_target_pairs={{4,0},{8,4},{12,8},{0,12},{5,1},{9,5},{13,9},{1,13},{6,2},{10,6},{... | collective-permute-start | bytes 2654216 | tf_op jit(solution)/shard_map/ppermute | solution.py:319
  229.2 22.1 %collective-permute-start.40 = (bf16[144,3072]{1,0:T(8,128)(2,1)S(1)}, bf16[144,3072]{1,0:T(8,128)(2,1)S(1)}, u32[]{:S(2)}, u32[]{:S(2)}) collective-permute-start(bf16[144,3072]{1,0:T(8,128)(2,1)S(1)} %add_convert_fusion.2), channel_id=1, source_target_pairs={{0,4},{4,8},{8,12},{12,0},{1,5},{5,9},{9,13},{13,1},{2,6},{6,10},{... | collective-permute-start | bytes 2654216 | tf_op jit(solution)/shard_map/ppermute | solution.py:319
  229.2 24.5 %collective-permute-start.32 = (bf16[144,3072]{1,0:T(8,128)(2,1)S(1)}, bf16[144,3072]{1,0:T(8,128)(2,1)S(1)}, u32[]{:S(2)}, u32[]{:S(2)}) collective-permute-start(bf16[144,3072]{1,0:T(8,128)(2,1)S(1)} %get-tuple-element.36), channel_id=1, source_target_pairs={{0,1},{1,0},{2,3},{3,2},{4,5},{5,4},{6,7},{7,6},{8,9},{9,8},{10,11... | collective-permute-start | bytes 2654216 | tf_op jit(solution)/shard_map/ppermute | solution.py:313
  230.0 23.8 %collective-permute-start.36 = (bf16[144,3072]{1,0:T(8,128)(2,1)S(1)}, bf16[144,3072]{1,0:T(8,128)(2,1)S(1)}, u32[]{:S(2)}, u32[]{:S(2)}) collective-permute-start(bf16[144,3072]{1,0:T(8,128)(2,1)S(1)} %add_convert_fusion.5), channel_id=1, source_target_pairs={{0,2},{2,0},{1,3},{3,1},{4,6},{6,4},{5,7},{7,5},{8,10},{10,8},{9,1... | collective-permute-start | bytes 2654216 | tf_op jit(solution)/shard_map/ppermute | solution.py:337
  252.6 21.7 %collective-permute-start.42 = (bf16[144,3072]{1,0:T(8,128)(2,1)}, bf16[144,3072]{1,0:T(8,128)(2,1)S(1)}, u32[]{:S(2)}, u32[]{:S(2)}) collective-permute-start(bf16[144,3072]{1,0:T(8,128)(2,1)} %add_convert_fusion.1), channel_id=1, source_target_pairs={{0,2},{2,0},{1,3},{3,1},{4,6},{6,4},{5,7},{7,5},{8,10},{10,8},{9,1... | collective-permute-start | bytes 2654216 | tf_op jit(solution)/shard_map/ppermute | solution.py:338
  253.8 1.7 copy-start.5
  255.1 21.4 %collective-permute-start.41 = (bf16[144,3072]{1,0:T(8,128)(2,1)}, bf16[144,3072]{1,0:T(8,128)(2,1)}, u32[]{:S(2)}, u32[]{:S(2)}) collective-permute-start(bf16[144,3072]{1,0:T(8,128)(2,1)} %add_convert_fusion.4), channel_id=1, source_target_pairs={{0,8},{4,12},{8,0},{12,4},{1,9},{5,13},{9,1},{13,5},{2,10},{6,14},... | collective-permute-start | bytes 2654216 | tf_op jit(solution)/shard_map/ppermute | solution.py:339
  280.5 18.9 %all-to-all-start.3 = ((bf16[8,18,3072]{2,1,0:T(8,128)(2,1)}), bf16[8,18,3072]{2,1,0:T(8,128)(2,1)S(1)}, u32[]{:S(2)}, u32[]{:S(2)}) async-start(bf16[8,18,3072]{2,1,0:T(8,128)(2,1)} %reshape.150), calls=%async_computation.3 | async-start | bytes 2359296 | tf_op jit(solution)/shard_map/all_to_all | solution.py:405
  284.1 3.4 %collective-permute-start.12 = (f32[32,2]{0,1:T(2,128)S(1)}, f32[32,2]{0,1:T(2,128)S(1)}, u32[]{:S(2)}, u32[]{:S(2)}) collective-permute-start(f32[32,2]{0,1:T(2,128)S(1)} %pad_maximum_fusion.7), channel_id=1, source_target_pairs={{0,1},{1,0},{2,3},{3,2},{4,5},{5,4},{6,7},{7,6},{8,9},{9,8},{10,11... | collective-permute-start | bytes 776 | tf_op jit(solution)/shard_map/ppermute | solution.py:397
  299.7 4.8 %copy-start.3 = (bf16[32,6144]{1,0:T(8,128)(2,1)S(1)}, bf16[32,6144]{1,0:T(8,128)(2,1)}, u32[]{:S(2)}) copy-start(bf16[32,6144]{1,0:T(8,128)(2,1)} %param.12) | copy-start | bytes 1179652
  300.3 4.2 %collective-permute-start.43 = (f32[32,3072]{1,0:T(8,128)S(1)}, f32[32,3072]{1,0:T(8,128)S(1)}, u32[]{:S(2)}, u32[]{:S(2)}) collective-permute-start(f32[32,3072]{1,0:T(8,128)S(1)} %get-tuple-element.46), channel_id=1, source_target_pairs={{0,1},{1,0},{2,3},{3,2},{4,5},{5,4},{6,7},{7,6},{8,9},{9,8},{10,11... | collective-permute-start | bytes 1179656 | tf_op jit(solution)/shard_map/ppermute | solution.py:411
  (9 other events, 9.8 us)
Sparse Core Ops, SparseCore 0:
  25.1 35.8 all-gather.1

commit v2 on v1

--- a/solution.py
+++ b/solution.py
@@ -301,7 +301,6 @@
 
 
 def experts_of(own, w_gate, w_up, w_down):
-    cut = own.shape[0] // 32 * 16
     c = lax.axis_index("c").astype(jnp.int32).reshape(1)
 
     def run(*blocks):
@@ -318,26 +317,27 @@
     def near_back(below, above):
         return lax.ppermute(below, "z", DOWN), lax.ppermute(above, "z", UP)
 
-    rest = own.shape[0] - cut
     over = lax.ppermute(own, "yh", SWAP)
     below, above = near(own)
-    up = lax.ppermute(jnp.concatenate([below[:cut], over], axis=0), "z", UP)
-    down = lax.ppermute(jnp.concatenate([above[cut:], over], axis=0), "z", DOWN)
-    far_own = jnp.concatenate([up[:cut], down[:rest]], axis=0)
-    over_below, over_above = up[cut:], down[rest:]
+    over_below = lax.ppermute(over, "z", UP)
+    far_own = lax.ppermute(above, "z", DOWN)
+    over_above = lax.ppermute(above, "yh", SWAP)
     far_over = lax.ppermute(far_own, "yh", SWAP)
-    own, over, below, above = summed(run(own, over, below, above))
+    parts = after(run(own, over, below, above), far_own, over_below, over_above)
+    own, over, below, above = summed(parts)
     own_back = near_back(below, above)
     parts = run(after(far_own, own, over, below, above), over_below, over_above)
     far_over = after(far_over, *own_back, parts[1][-1])
-    last = run(far_over)
     far_own, over_below, over_above = summed(parts)
     over_back = near_back(over_below, over_above)
-    (far_over,) = summed(last)
-    far_own = add(far_own, lax.ppermute(far_over, "yh", SWAP))
+    last = run(after(far_over, over_below, over_above))
+    (last_sum,) = summed(last)
+    far_over = lax.ppermute(
+        last_sum, ("z", "yh"), [(NYH * a + i, NYH * b + 1 - i) for a, b in FAR for i in range(NYH)]
+    )
+    far_own = lax.ppermute(after(far_own, *over_back), "z", FAR)
     over = lax.ppermute(add(over, *over_back), "yh", SWAP)
-    far_own = lax.ppermute(after(far_own, *over_back), "z", FAR)
-    return add(own, *own_back, far_own, over)
+    return add(own, *own_back, far_own, far_over, over)
 
 
 def per_device(

time: 317 us -> 316 us (level)
  local copies, waits for them, and re-layouts: 14.2 us -> 9.72 us
    ppermute x1, waiting for transfers between devices: 18.3 us -> 1.35 us  [experts_of(): over = lax.ppermute(add(over, *over_back), 'yh', SWAP)]
    ppermute x3 -> x4, waiting for transfers between devices: 5.37 us -> 21.4 us  [the longest x1 21.4 us: experts_of(): lax.ppermute(last_sum, ('z', 'yh'), [(NYH * a + i, NYH * b + 1 - i) for a...]
    ppermute x4, waiting for transfers between devices: 21.6 us -> 9.46 us  [near_back(): return (lax.ppermute(below, 'z', DOWN), lax.ppermute(above, 'z', UP))]
    ppermute x1, waiting for transfers between devices: 1.34 us -> 12.6 us  [experts_of(): far_own = lax.ppermute(after(far_own, *over_back), 'z', FAR)]
    ppermute x3 -> x4, starting transfers between devices: 3.51 us -> 8.53 us  [the longest x1 4.08 us: experts_of(): lax.ppermute(last_sum, ('z', 'yh'), [(NYH * a + i, NYH * b + 1 - i) for a...]
    ppermute x8, waiting for transfers between devices: 0.02 us -> 4.68 us  [summed(): lax.ppermute(his, 'c', SWAP)]
    unnamed x50, local copies, waits for them, and re-layouts: 6.29 us -> 2.92 us
  transfers between devices with their start and end apart: 48 -> 49, of which waited for: 23 -> 25; matrix products, arithmetic and copies ran while one was open for 3% -> 4% of each run, Pallas kernels for 16% -> 16%
where the time goes in v2:
time: 316 us; the launch traced here: 312 us
  waiting for transfers between devices  112 us (35%)
  starting transfers between devices  86.1 us (27%)
  Pallas kernels  50.3 us (16%)
  blocking collectives  18.6 us (6%)
  other arithmetic  16.1 us (5%)
  between operations  14.2 us (4%)
  local copies, waits for them, and re-layouts  9.72 us (3%)
  matrix products  4.42 us (1%)
    pallas_call x3, Pallas kernels, expert_part(): pl.pallas_call(functools.partial(expert_kernel, count), grid_spec=pltpu.P...  45.9 us
    ppermute x1, waiting for transfers between devices, experts_of(): lax.ppermute(last_sum, ('z', 'yh'), [(NYH * a + i, NYH * b + 1 - i) for a...  21.4 us
    all_to_all x1, blocking collectives, per_device(): lax.all_to_all(packed.reshape(experts, cap, half), ('x', 'yl'), split_axi...  18.6 us
    ppermute x4, starting transfers between devices, near_back(): return (lax.ppermute(below, 'z', DOWN), lax.ppermute(above, 'z', UP))  15 us
    ppermute x1, waiting for transfers between devices, experts_of(): over = lax.ppermute(own, 'yh', SWAP)  14 us
    ppermute x1, waiting for transfers between devices, experts_of(): far_own = lax.ppermute(after(far_own, *over_back), 'z', FAR)  12.6 us
    ppermute x4, starting transfers between devices, over_ctx(): return lax.ppermute(array, ('x', 'yl'), route)  10.9 us
    all_to_all x1, waiting for transfers between devices, project(): lax.all_to_all(part.reshape(NZ * NYH, rows, width), ('z', 'yh'), split_ax...  10.8 us
  transfers between devices with their start and end apart: 49, of which 25 were waited for; matrix products, arithmetic and copies ran while one was open for 4% of the time, Pallas kernels for 16%

profile of v2, /device:TPU:1, one launch (start us, length us, event | category | flops | bytes accessed | tf_op | source)
XLA Modules:
  0.0 311.8 jit_solution(6308569611412052799)
XLA Ops:
  6.5 2.2 collective-permute-start.9
  10.3 4.6 %collective-permute-start = (bf16[272,128]{1,0:T(8,128)(2,1)S(1)}, bf16[272,128]{1,0:T(8,128)(2,1)S(1)}, u32[]{:S(2)}, u32[]{:S(2)}) collective-permute-start(bf16[272,128]{1,0:T(8,128)(2,1)S(1)} %fusion.11.own), channel_id=1, source_target_pairs={{0,64},{16,80},{32,96},{48,112},{1,65},{17,81},{33,97},{49,113},{2... | collective-permute-start | bytes 208904 | tf_op jit(solution)/shard_map/ppermute | solution.py:36
  14.9 2.1 collective-permute-start.1
  17.0 2.3 collective-permute-start.2
  19.3 1.8 collective-permute-start.3
  21.2 1.9 collective-permute-done.3
  23.1 1.0 broadcast_select_fusion.1
  25.1 1.7 collective-permute-start.4
  26.8 2.2 collective-permute-start.5
  29.0 5.1 %collective-permute-done.4.below = bf16[1088,128]{1,0:T(8,128)(2,1)S(1)} collective-permute-done((bf16[1088,128]{1,0:T(8,128)(2,1)S(1)}, bf16[1088,128]{1,0:T(8,128)(2,1)S(1)}, u32[]{:S(2)}, u32[]{:S(2)}) %collective-permute-start.4) | collective-permute-done | bytes 278560 | tf_op jit(solution)/shard_map/ppermute | solution.py:51
  34.2 2.3 collective-permute-start.8
  37.6 2.2 collective-permute-done.8.far
  40.1 4.4 %attention.1 = bf16[128,768]{1,0:T(8,128)(2,1)S(1)} custom-call(s32[17]{0:T(128)S(1)} %stack.76.base, bf16[128,768]{1,0:T(8,128)(2,1)S(1)} %copy-done.1, f32[128,1]{1,0:T(8,128)S(1)} %copy.39.query_doc, bf16[272,128]{1,0:T(8,128)(2,1)S(1)} %fusion.11.own, bf16[272,128]{1,0:T(8,128)(2,1)S(1)} %collective-permute-done.two, ...), custom_call_target="tpu_custom_call" | custom-call | flops 905969664 | bytes 1179648 | tf_op jit(solution)/shard_map/attention/pallas_call | solution.py:146
  44.5 0.9 broadcast_in_dim.48
  45.5 3.5 %all-to-all-start = ((bf16[4,128,768]{2,1,0:T(8,128)(2,1)}), bf16[4,128,768]{2,1,0:T(8,128)(2,1)S(1)}, u32[]{:S(2)}, u32[]{:S(2)}) async-start(bf16[4,128,768]{2,1,0:T(8,128)(2,1)} %broadcast_in_dim.48), calls=%async_computation | async-start | bytes 1572864 | tf_op jit(solution)/shard_map/all_to_all | solution.py:186
  49.0 8.4 %all-to-all-done = bf16[4,128,768]{2,1,0:T(8,128)(2,1)S(1)} async-done(((bf16[4,128,768]{2,1,0:T(8,128)(2,1)}), bf16[4,128,768]{2,1,0:T(8,128)(2,1)S(1)}, u32[]{:S(2)}, u32[]{:S(2)}) %all-to-all-start) | async-done | bytes 786464 | tf_op jit(solution)/shard_map/all_to_all | solution.py:186
  57.3 3.7 %all-gather.2.cloned.1.call-done = bf16[1536,768]{1,0:T(8,128)(2,1)} async-done(((bf16[384,768]{1,0:T(8,128)(2,1)}), bf16[1536,768]{1,0:T(8,128)(2,1)}) %all-gather.2.cloned.1.call-update) | async-done | bytes 2359312 | tf_op jit(solution)/shard_map/all_gather | solution.py:177
  61.0 3.1 convolution_convert_fusion.1
  64.2 1.7 collective-permute-start.10
  65.8 1.9 collective-permute-done.10
  67.7 1.1 fusion
  68.9 5.7 %all-to-all-start.1 = ((bf16[8,32,1536]{2,1,0:T(8,128)(2,1)}), bf16[8,32,1536]{2,1,0:T(8,128)(2,1)S(1)}, u32[]{:S(2)}, u32[]{:S(2)}) async-start(bf16[8,32,1536]{2,1,0:T(8,128)(2,1)} %bitcast.24), calls=%async_computation.1 | async-start | bytes 1572864 | tf_op jit(solution)/shard_map/all_to_all | solution.py:197
  77.3 10.8 %all-to-all-done.1 = bf16[8,32,1536]{2,1,0:T(8,128)(2,1)S(1)} async-done(((bf16[8,32,1536]{2,1,0:T(8,128)(2,1)}), bf16[8,32,1536]{2,1,0:T(8,128)(2,1)S(1)}, u32[]{:S(2)}, u32[]{:S(2)}) %all-to-all-start.1) | async-done | bytes 786464 | tf_op jit(solution)/shard_map/all_to_all | solution.py:197
  89.7 0.9 reshape.146
  91.2 1.9 collective-permute-start.13
  94.9 18.6 %all_to_all.20 = bf16[8,18,3072]{2,1,0:T(8,128)(2,1)S(1)} all-to-all(bf16[8,18,3072]{2,1,0:T(8,128)(2,1)S(1)} %reshape.148), channel_id=1, replica_groups=mesh['x'=4,'yl'=2,'z'=4,'yh'=2,'c'=2] {'x','yl'}, dimensions={0} | all-to-all | bytes 1769472 | tf_op jit(solution)/shard_map/all_to_all | solution.py:401
  113.8 1.3 collective-permute-start.14
  115.6 2.4 collective-permute-start.16
  118.0 2.7 collective-permute-start.17
  120.7 14.0 %collective-permute-done.14.refs_1_ = bf16[144,3072]{1,0:T(8,128)(2,1)S(1)} collective-permute-done((bf16[144,3072]{1,0:T(8,128)(2,1)S(1)}, bf16[144,3072]{1,0:T(8,128)(2,1)S(1)}, u32[]{:S(2)}, u32[]{:S(2)}) %collective-permute-start.14) | collective-permute-done | bytes 884768 | tf_op jit(solution)/shard_map/ppermute | solution.py:320
  134.6 2.8 collective-permute-start.18
  137.4 1.1 collective-permute-start.19
  138.7 2.6 collective-permute-start.21
  141.3 1.9 collective-permute-start.23
  144.1 1.0 copy-done.24
  145.1 19.2 %expert_part.3 = (bf16[144,3072]{1,0:T(8,128)(2,1)S(1)}, bf16[144,3072]{1,0:T(8,128)(2,1)S(1)}, bf16[144,3072]{1,0:T(8,128)(2,1)S(1)}, bf16[144,3072]{1,0:T(8,12...) custom-call(s32[1]{0:T(128)} %bitcast.29.core_ref, ...), custom_call_target="tpu_custom_call" | custom-call | flops 10871635968 | bytes 33030144 | tf_op jit(solution)/shard_map/expert_part/pallas_call | solution.py:272
  166.1 1.0 collective-permute-done.27
  167.5 1.4 add_convert_fusion.7
  169.8 1.1 collective-permute-done.24
  171.6 1.7 collective-permute-start.39
  173.2 12.5 %collective-permute-start.26 = (bf16[144,3072]{1,0:T(8,128)(2,1)S(1)}, bf16[144,3072]{1,0:T(8,128)(2,1)S(1)}, u32[]{:S(2)}, u32[]{:S(2)}) collective-permute-start(bf16[144,3072]{1,0:T(8,128)(2,1)S(1)} %add_convert_fusion.8), channel_id=1, source_target_pairs={{4,0},{8,4},{12,8},{0,12},{5,1},{9,5},{13,9},{1,13},{6,2},{10,6},{... | collective-permute-start | bytes 2654216 | tf_op jit(solution)/shard_map/ppermute | solution.py:318
  185.7 0.9 copy-done.20
  186.7 15.7 %expert_part.4 = (bf16[144,3072]{1,0:T(8,128)(2,1)S(1)}, bf16[144,3072]{1,0:T(8,128)(2,1)S(1)}, bf16[144,3072]{1,0:T(8,128)(2,1)S(1)}, bf16[144,3072]{1,0:T(8,12...) custom-call(s32[1]{0:T(128)} %bitcast.29.core_ref, ...), custom_call_target="tpu_custom_call" | custom-call | flops 8153726976 | bytes 29491200 | tf_op jit(solution)/shard_map/expert_part/pallas_call | solution.py:272
  204.3 1.0 collective-permute-done.36
  205.5 1.0 collective-permute-done.34
  207.4 2.5 collective-permute-start.35
  209.9 11.0 %expert_part.5 = (bf16[144,3072]{1,0:T(8,128)(2,1)S(1)}, bf16[144,3072]{1,0:T(8,128)(2,1)S(1)}) custom-call(s32[1]{0:T(128)} %bitcast.29.core_ref, bf16[144,3072]{1,0:T(8,128)(2,1)S(1)} %collective-permute-done.39.refs_0_, bf16[144,3072]{1,0:T(8,128)(2,1)S(1)} %collective-permute-done.40.refs_1_, bf16[6144,512]{1,0:T(8,128)(2,1)} %refs_2_.1, ...), custom_call_target="tpu_custom_call" | custom-call | flops 2717908992 | bytes 22413312 | tf_op jit(solution)/shard_map/expert_part/pallas_call | solution.py:272
  221.8 1.1 add_convert_fusion.5
  223.0 5.4 %collective-permute-done.35 = bf16[144,3072]{1,0:T(8,128)(2,1)S(1)} collective-permute-done((bf16[144,3072]{1,0:T(8,128)(2,1)S(1)}, bf16[144,3072]{1,0:T(8,128)(2,1)S(1)}, u32[]{:S(2)}, u32[]{:S(2)}) %collective-permute-start.35) | collective-permute-done | bytes 884768 | tf_op jit(solution)/shard_map/ppermute | solution.py:318
  228.4 3.1 collective-permute-done.37
  231.5 1.4 add_convert_fusion.1
  232.9 1.6 collective-permute-start.43
  234.5 1.2 add_convert_fusion.2
  235.6 4.1 %collective-permute-start.42 = (bf16[144,3072]{1,0:T(8,128)(2,1)}, bf16[144,3072]{1,0:T(8,128)(2,1)}, u32[]{:S(2)}, u32[]{:S(2)}) collective-permute-start(bf16[144,3072]{1,0:T(8,128)(2,1)} %add_convert_fusion.2), channel_id=1, source_target_pairs={{0,10},{2,8},{4,14},{6,12},{8,2},{10,0},{12,6},{14,4},{1,11},{3,9}... | collective-permute-start | bytes 2654216 | tf_op jit(solution)/shard_map/ppermute | solution.py:335
  240.2 12.6 %collective-permute-done.38 = bf16[144,3072]{1,0:T(8,128)(2,1)S(1)} collective-permute-done((bf16[144,3072]{1,0:T(8,128)(2,1)}, bf16[144,3072]{1,0:T(8,128)(2,1)S(1)}, u32[]{:S(2)}, u32[]{:S(2)}) %collective-permute-start.38) | collective-permute-done | bytes 884768 | tf_op jit(solution)/shard_map/ppermute | solution.py:338
  252.8 1.4 collective-permute-done.43
  254.2 21.4 %collective-permute-done.42 = bf16[144,3072]{1,0:T(8,128)(2,1)} collective-permute-done((bf16[144,3072]{1,0:T(8,128)(2,1)}, bf16[144,3072]{1,0:T(8,128)(2,1)}, u32[]{:S(2)}, u32[]{:S(2)}) %collective-permute-start.42) | collective-permute-done | bytes 884768 | tf_op jit(solution)/shard_map/ppermute | solution.py:335
  275.5 3.1 add_convert_fusion
  278.6 1.3 reshape.150
  279.9 3.6 %all-to-all-start.3 = ((bf16[8,18,3072]{2,1,0:T(8,128)(2,1)}), bf16[8,18,3072]{2,1,0:T(8,128)(2,1)S(1)}, u32[]{:S(2)}, u32[]{:S(2)}) async-start(bf16[8,18,3072]{2,1,0:T(8,128)(2,1)} %reshape.150), calls=%async_computation.3 | async-start | bytes 2359296 | tf_op jit(solution)/shard_map/all_to_all | solution.py:405
  283.5 3.0 collective-permute-start.12
  287.8 10.6 %all-to-all-done.3 = bf16[8,18,3072]{2,1,0:T(8,128)(2,1)S(1)} async-done(((bf16[8,18,3072]{2,1,0:T(8,128)(2,1)}), bf16[8,18,3072]{2,1,0:T(8,128)(2,1)S(1)}, u32[]{:S(2)}, u32[]{:S(2)}) %all-to-all-start.3) | async-done | bytes 884768 | tf_op jit(solution)/shard_map/all_to_all | solution.py:405
  299.3 3.2 %collective-permute-start.44 = (f32[32,3072]{1,0:T(8,128)S(1)}, f32[32,3072]{1,0:T(8,128)S(1)}, u32[]{:S(2)}, u32[]{:S(2)}) collective-permute-start(f32[32,3072]{1,0:T(8,128)S(1)} %get-tuple-element.64), channel_id=1, source_target_pairs={{0,1},{1,0},{2,3},{3,2},{4,5},{5,4},{6,7},{7,6},{8,9},{9,8},{10,11... | collective-permute-start | bytes 1179656 | tf_op jit(solution)/shard_map/ppermute | solution.py:411
  302.5 1.3 collective-permute-done.44
  (153 shorter events, 23.3 us)
Async XLA Ops:
  6.5 233.2 %copy-start = (f32[6144,8]{0,1:T(8,128)S(1)}, f32[6144,8]{0,1:T(8,128)}, u32[]{:S(2)}) copy-start(f32[6144,8]{0,1:T(8,128)} %param.19) | copy-start | bytes 589828
  6.5 18.5 %copy-start.11 = (bf16[128,128]{1,0:T(8,128)(2,1)S(1)}, bf16[128,128]{1,0:T(8,128)(2,1)}, u32[]{:S(2)}) copy-start(bf16[128,128]{1,0:T(8,128)(2,1)} %param.14) | copy-start | bytes 98308
  6.5 18.5 %copy-start.10 = (bf16[128,128]{1,0:T(8,128)(2,1)S(1)}, bf16[128,128]{1,0:T(8,128)(2,1)}, u32[]{:S(2)}) copy-start(bf16[128,128]{1,0:T(8,128)(2,1)} %param.15) | copy-start | bytes 98308
  6.5 54.5 %all-gather.2.cloned.1.call-start = ((), (), s32[]{:S(2)}) async-start(), calls=%async_computation.4 | async-start | bytes 2949120 | tf_op jit(solution)/shard_map/all_gather | solution.py:177
  6.5 16.6 %collective-permute-start.9 = (bf16[192,768]{1,0:T(8,128)(2,1)}, bf16[192,768]{1,0:T(8,128)(2,1)S(1)}, u32[]{:S(2)}, u32[]{:S(2)}) collective-permute-start(bf16[192,768]{1,0:T(8,128)(2,1)} %bitcast.51), channel_id=1, source_target_pairs={{0,16},{16,0},{1,17},{17,1},{2,18},{18,2},{3,19},{19,3},{4,20},{20... | collective-permute-start | bytes 884744 | tf_op jit(solution)/shard_map/ppermute | solution.py:174
  10.3 10.9 %collective-permute-start = (bf16[272,128]{1,0:T(8,128)(2,1)S(1)}, bf16[272,128]{1,0:T(8,128)(2,1)S(1)}, u32[]{:S(2)}, u32[]{:S(2)}) collective-permute-start(bf16[272,128]{1,0:T(8,128)(2,1)S(1)} %fusion.11.own), channel_id=1, source_target_pairs={{0,64},{16,80},{32,96},{48,112},{1,65},{17,81},{33,97},{49,113},{2... | collective-permute-start | bytes 208904 | tf_op jit(solution)/shard_map/ppermute | solution.py:36
  14.9 6.3 %collective-permute-start.1 = (bf16[272,128]{1,0:T(8,128)(2,1)S(1)}, bf16[272,128]{1,0:T(8,128)(2,1)S(1)}, u32[]{:S(2)}, u32[]{:S(2)}) collective-permute-start(bf16[272,128]{1,0:T(8,128)(2,1)S(1)} %fusion.11.own), channel_id=1, source_target_pairs={{0,16},{16,64},{32,48},{48,96},{64,80},{96,112},{1,17},{17,65},{33... | collective-permute-start | bytes 208904 | tf_op jit(solution)/shard_map/ppermute | solution.py:36
  17.0 4.2 %collective-permute-start.2 = (bf16[272,128]{1,0:T(8,128)(2,1)S(1)}, bf16[272,128]{1,0:T(8,128)(2,1)S(1)}, u32[]{:S(2)}, u32[]{:S(2)}) collective-permute-start(bf16[272,128]{1,0:T(8,128)(2,1)S(1)} %fusion.11.own), channel_id=1, source_target_pairs={{0,48},{16,32},{32,80},{48,64},{64,112},{80,96},{1,49},{17,33},{33... | collective-permute-start | bytes 208904 | tf_op jit(solution)/shard_map/ppermute | solution.py:36
  19.3 3.8 %collective-permute-start.3 = (bf16[272,128]{1,0:T(8,128)(2,1)S(1)}, bf16[272,128]{1,0:T(8,128)(2,1)S(1)}, u32[]{:S(2)}, u32[]{:S(2)}) collective-permute-start(bf16[272,128]{1,0:T(8,128)(2,1)S(1)} %fusion.11.own), channel_id=1, source_target_pairs={{0,32},{16,48},{32,64},{48,80},{64,96},{80,112},{1,33},{17,49},{33... | collective-permute-start | bytes 208904 | tf_op jit(solution)/shard_map/ppermute | solution.py:36
  24.1 16.0 %copy-start.1 = (bf16[128,768]{1,0:T(8,128)(2,1)S(1)}, bf16[128,768]{1,0:T(8,128)(2,1)}, u32[]{:S(2)}) copy-start(bf16[128,768]{1,0:T(8,128)(2,1)} %query.1) | copy-start | bytes 589828
  25.1 9.0 %collective-permute-start.4 = (bf16[1088,128]{1,0:T(8,128)(2,1)S(1)}, bf16[1088,128]{1,0:T(8,128)(2,1)S(1)}, u32[]{:S(2)}, u32[]{:S(2)}) collective-permute-start(bf16[1088,128]{1,0:T(8,128)(2,1)S(1)} %get-tuple-element.70.mid), channel_id=1, source_target_pairs={{0,4},{4,8},{8,12},{12,0},{1,5},{5,9},{9,13},{13,1},{2,6},{6,10},{... | collective-permute-start | bytes 835592 | tf_op jit(solution)/shard_map/ppermute | solution.py:51
  26.8 9.8 %collective-permute-start.5 = (bf16[1088,128]{1,0:T(8,128)(2,1)S(1)}, bf16[1088,128]{1,0:T(8,128)(2,1)S(1)}, u32[]{:S(2)}, u32[]{:S(2)}) collective-permute-start(bf16[1088,128]{1,0:T(8,128)(2,1)S(1)} %get-tuple-element.69), channel_id=1, source_target_pairs={{4,0},{8,4},{12,8},{0,12},{5,1},{9,5},{13,9},{1,13},{6,2},{10,6},{... | collective-permute-start | bytes 835592 | tf_op jit(solution)/shard_map/ppermute | solution.py:52
  34.2 5.9 %collective-permute-start.6 = (bf16[544,128]{1,0:T(8,128)(2,1)S(1)}, bf16[544,128]{1,0:T(8,128)(2,1)S(1)}, u32[]{:S(2)}, u32[]{:S(2)}) collective-permute-start(bf16[544,128]{1,0:T(8,128)(2,1)S(1)} %slice.26), channel_id=1, source_target_pairs={{0,4},{4,8},{8,12},{12,0},{1,5},{5,9},{9,13},{13,1},{2,6},{6,10},{... | collective-permute-start | bytes 417800 | tf_op jit(solution)/shard_map/ppermute | solution.py:54
  34.2 5.6 %collective-permute-start.8 = (bf16[272,128]{1,0:T(8,128)(2,1)S(1)}, bf16[272,128]{1,0:T(8,128)(2,1)S(1)}, u32[]{:S(2)}, u32[]{:S(2)}) collective-permute-start(bf16[272,128]{1,0:T(8,128)(2,1)S(1)} %get-tuple-element.71), channel_id=1, source_target_pairs={{0,8},{4,12},{8,0},{12,4},{1,9},{5,13},{9,1},{13,5},{2,10},{6,14},... | collective-permute-start | bytes 208904 | tf_op jit(solution)/shard_map/ppermute | solution.py:53
  36.6 3.3 %collective-permute-start.7 = (bf16[272,128]{1,0:T(8,128)(2,1)S(1)}, bf16[272,128]{1,0:T(8,128)(2,1)S(1)}, u32[]{:S(2)}, u32[]{:S(2)}) collective-permute-start(bf16[272,128]{1,0:T(8,128)(2,1)S(1)} %slice.27), channel_id=1, source_target_pairs={{4,0},{8,4},{12,8},{0,12},{5,1},{9,5},{13,9},{1,13},{6,2},{10,6},{... | collective-permute-start | bytes 208904 | tf_op jit(solution)/shard_map/ppermute | solution.py:55
  45.5 11.9 %all-to-all-start = ((bf16[4,128,768]{2,1,0:T(8,128)(2,1)}), bf16[4,128,768]{2,1,0:T(8,128)(2,1)S(1)}, u32[]{:S(2)}, u32[]{:S(2)}) async-start(bf16[4,128,768]{2,1,0:T(8,128)(2,1)} %broadcast_in_dim.48), calls=%async_computation | async-start | bytes 1572864 | tf_op jit(solution)/shard_map/all_to_all | solution.py:186
  64.2 3.6 %collective-permute-start.10 = (bf16[4,2,32,1536]{3,2,1,0:T(8,128)(2,1)S(1)}, bf16[4,2,32,1536]{3,2,1,0:T(8,128)(2,1)S(1)}, u32[]{:S(2)}, u32[]{:S(2)}) collective-permute-start(bf16[4,2,32,1536]{3,2,1,0:T(8,128)(2,1)S(1)} %dynamic-slice_bitcast_fusion), channel_id=1, source_target_pairs={{0,1},{1,0},{2,3},{3,2},{4,5},{5,4},{6,7},{7,6},{8,9},{9,8},{10,11... | collective-permute-start | bytes 2359304 | tf_op jit(solution)/shard_map/ppermute | solution.py:195
  65.8 8.7 %copy-start.13 = (s32[32,2]{0,1:T(2,128)S(1)}, s32[32,2]{0,1:T(2,128)}, u32[]{:S(2)}) copy-start(s32[32,2]{0,1:T(2,128)} %param.23) | copy-start | bytes 772
  68.9 19.2 %all-to-all-start.1 = ((bf16[8,32,1536]{2,1,0:T(8,128)(2,1)}), bf16[8,32,1536]{2,1,0:T(8,128)(2,1)S(1)}, u32[]{:S(2)}, u32[]{:S(2)}) async-start(bf16[8,32,1536]{2,1,0:T(8,128)(2,1)} %bitcast.24), calls=%async_computation.1 | async-start | bytes 1572864 | tf_op jit(solution)/shard_map/all_to_all | solution.py:197
  74.6 1.6 collective-permute-start.11
  91.2 3.0 collective-permute-start.13
  113.8 31.3 %copy-start.9 = (bf16[144,3072]{1,0:T(8,128)(2,1)}, bf16[144,3072]{1,0:T(8,128)(2,1)S(1)}, u32[]{:S(2)}) copy-start(bf16[144,3072]{1,0:T(8,128)(2,1)S(1)} %reshape.149.refs_0_) | copy-start | bytes 2654212
  113.8 20.9 %collective-permute-start.14 = (bf16[144,3072]{1,0:T(8,128)(2,1)S(1)}, bf16[144,3072]{1,0:T(8,128)(2,1)S(1)}, u32[]{:S(2)}, u32[]{:S(2)}) collective-permute-start(bf16[144,3072]{1,0:T(8,128)(2,1)S(1)} %reshape.149.refs_0_), channel_id=1, source_target_pairs={{0,2},{2,0},{1,3},{3,1},{4,6},{6,4},{5,7},{7,5},{8,10},{10,8},{9,1... | collective-permute-start | bytes 2654216 | tf_op jit(solution)/shard_map/ppermute | solution.py:320
  115.1 22.4 %collective-permute-start.15 = (bf16[144,3072]{1,0:T(8,128)(2,1)S(1)}, bf16[144,3072]{1,0:T(8,128)(2,1)S(1)}, u32[]{:S(2)}, u32[]{:S(2)}) collective-permute-start(bf16[144,3072]{1,0:T(8,128)(2,1)S(1)} %reshape.149.refs_0_), channel_id=1, source_target_pairs={{0,4},{4,8},{8,12},{12,0},{1,5},{5,9},{9,13},{13,1},{2,6},{6,10},{... | collective-permute-start | bytes 2654216 | tf_op jit(solution)/shard_map/ppermute | solution.py:315
  115.6 23.0 %collective-permute-start.16 = (bf16[144,3072]{1,0:T(8,128)(2,1)S(1)}, bf16[144,3072]{1,0:T(8,128)(2,1)S(1)}, u32[]{:S(2)}, u32[]{:S(2)}) collective-permute-start(bf16[144,3072]{1,0:T(8,128)(2,1)S(1)} %reshape.149.refs_0_), channel_id=1, source_target_pairs={{4,0},{8,4},{12,8},{0,12},{5,1},{9,5},{13,9},{1,13},{6,2},{10,6},{... | collective-permute-start | bytes 2654216 | tf_op jit(solution)/shard_map/ppermute | solution.py:315
  118.0 23.3 %collective-permute-start.17 = (bf16[144,3072]{1,0:T(8,128)(2,1)S(1)}, bf16[144,3072]{1,0:T(8,128)(2,1)S(1)}, u32[]{:S(2)}, u32[]{:S(2)}) collective-permute-start(bf16[144,3072]{1,0:T(8,128)(2,1)S(1)} %reshape.149.refs_0_), channel_id=1, source_target_pairs={{0,1},{1,0},{2,3},{3,2},{4,5},{5,4},{6,7},{7,6},{8,9},{9,8},{10,11... | collective-permute-start | bytes 2654216 | tf_op jit(solution)/shard_map/ppermute | solution.py:307
  134.6 10.4 %copy-start.16 = (bf16[144,3072]{1,0:T(8,128)(2,1)}, bf16[144,3072]{1,0:T(8,128)(2,1)S(1)}, u32[]{:S(2)}) copy-start(bf16[144,3072]{1,0:T(8,128)(2,1)S(1)} %collective-permute-done.14.refs_1_) | copy-start | bytes 2654212
  134.6 6.6 %collective-permute-start.18 = (bf16[144,3072]{1,0:T(8,128)(2,1)S(1)}, bf16[144,3072]{1,0:T(8,128)(2,1)S(1)}, u32[]{:S(2)}, u32[]{:S(2)}) collective-permute-start(bf16[144,3072]{1,0:T(8,128)(2,1)S(1)} %collective-permute-done.14.refs_1_), channel_id=1, source_target_pairs={{0,1},{1,0},{2,3},{3,2},{4,5},{5,4},{6,7},{7,6},{8,9},{9,8},{10,11... | collective-permute-start | bytes 2654216 | tf_op jit(solution)/shard_map/ppermute | solution.py:307
  137.4 7.6 %copy-start.19 = (bf16[144,3072]{1,0:T(8,128)(2,1)}, bf16[144,3072]{1,0:T(8,128)(2,1)S(1)}, u32[]{:S(2)}) copy-start(bf16[144,3072]{1,0:T(8,128)(2,1)S(1)} %collective-permute-done.15.refs_2_) | copy-start | bytes 2654212
  137.4 5.7 %collective-permute-start.19 = (bf16[144,3072]{1,0:T(8,128)(2,1)S(1)}, bf16[144,3072]{1,0:T(8,128)(2,1)S(1)}, u32[]{:S(2)}, u32[]{:S(2)}) collective-permute-start(bf16[144,3072]{1,0:T(8,128)(2,1)S(1)} %collective-permute-done.15.refs_2_), channel_id=1, source_target_pairs={{0,1},{1,0},{2,3},{3,2},{4,5},{5,4},{6,7},{7,6},{8,9},{9,8},{10,11... | collective-permute-start | bytes 2654216 | tf_op jit(solution)/shard_map/ppermute | solution.py:307
  138.6 6.5 %copy-start.17 = (bf16[144,3072]{1,0:T(8,128)(2,1)}, bf16[144,3072]{1,0:T(8,128)(2,1)S(1)}, u32[]{:S(2)}) copy-start(bf16[144,3072]{1,0:T(8,128)(2,1)S(1)} %collective-permute-done.16.refs_3_) | copy-start | bytes 2654212
  138.6 4.6 %collective-permute-start.20 = (bf16[144,3072]{1,0:T(8,128)(2,1)S(1)}, bf16[144,3072]{1,0:T(8,128)(2,1)S(1)}, u32[]{:S(2)}, u32[]{:S(2)}) collective-permute-start(bf16[144,3072]{1,0:T(8,128)(2,1)S(1)} %collective-permute-done.16.refs_3_), channel_id=1, source_target_pairs={{0,1},{1,0},{2,3},{3,2},{4,5},{5,4},{6,7},{7,6},{8,9},{9,8},{10,11... | collective-permute-start | bytes 2654216 | tf_op jit(solution)/shard_map/ppermute | solution.py:307
  138.7 25.6 %collective-permute-start.21 = (bf16[144,3072]{1,0:T(8,128)(2,1)S(1)}, bf16[144,3072]{1,0:T(8,128)(2,1)S(1)}, u32[]{:S(2)}, u32[]{:S(2)}) collective-permute-start(bf16[144,3072]{1,0:T(8,128)(2,1)S(1)} %collective-permute-done.16.refs_3_), channel_id=1, source_target_pairs={{4,0},{8,4},{12,8},{0,12},{5,1},{9,5},{13,9},{1,13},{6,2},{10,6},{... | collective-permute-start | bytes 2654216 | tf_op jit(solution)/shard_map/ppermute | solution.py:323
  141.3 3.8 %copy-start.21 = (bf16[144,3072]{1,0:T(8,128)(2,1)}, bf16[144,3072]{1,0:T(8,128)(2,1)S(1)}, u32[]{:S(2)}) copy-start(bf16[144,3072]{1,0:T(8,128)(2,1)S(1)} %collective-permute-done.17.refs_4_) | copy-start | bytes 2654212
  141.3 23.0 %collective-permute-start.22 = (bf16[144,3072]{1,0:T(8,128)(2,1)S(1)}, bf16[144,3072]{1,0:T(8,128)(2,1)S(1)}, u32[]{:S(2)}, u32[]{:S(2)}) collective-permute-start(bf16[144,3072]{1,0:T(8,128)(2,1)S(1)} %collective-permute-done.14.refs_1_), channel_id=1, source_target_pairs={{0,4},{4,8},{8,12},{12,0},{1,5},{5,9},{9,13},{13,1},{2,6},{6,10},{... | collective-permute-start | bytes 2654216 | tf_op jit(solution)/shard_map/ppermute | solution.py:322
  141.3 23.0 %collective-permute-start.23 = (bf16[144,3072]{1,0:T(8,128)(2,1)S(1)}, bf16[144,3072]{1,0:T(8,128)(2,1)S(1)}, u32[]{:S(2)}, u32[]{:S(2)}) collective-permute-start(bf16[144,3072]{1,0:T(8,128)(2,1)S(1)} %collective-permute-done.16.refs_3_), channel_id=1, source_target_pairs={{0,2},{2,0},{1,3},{3,1},{4,6},{6,4},{5,7},{7,5},{8,10},{10,8},{9,1... | collective-permute-start | bytes 2654216 | tf_op jit(solution)/shard_map/ppermute | solution.py:324
  164.3 4.8 %copy-start.14 = (bf16[144,3072]{1,0:T(8,128)(2,1)}, bf16[144,3072]{1,0:T(8,128)(2,1)S(1)}, u32[]{:S(2)}) copy-start(bf16[144,3072]{1,0:T(8,128)(2,1)S(1)} %collective-permute-done.22.refs_1_) | copy-start | bytes 2654212
  164.3 4.8 %copy-start.15 = (bf16[144,3072]{1,0:T(8,128)(2,1)}, bf16[144,3072]{1,0:T(8,128)(2,1)S(1)}, u32[]{:S(2)}) copy-start(bf16[144,3072]{1,0:T(8,128)(2,1)S(1)} %collective-permute-done.23.refs_2_) | copy-start | bytes 2654212
  164.3 2.8 collective-permute-start.27
  165.0 3.8 %collective-permute-start.25 = (bf16[144,3072]{1,0:T(8,128)(2,1)S(1)}, bf16[144,3072]{1,0:T(8,128)(2,1)S(1)}, u32[]{:S(2)}, u32[]{:S(2)}) collective-permute-start(bf16[144,3072]{1,0:T(8,128)(2,1)S(1)} %get-tuple-element.46), channel_id=1, source_target_pairs={{0,1},{1,0},{2,3},{3,2},{4,5},{5,4},{6,7},{7,6},{8,9},{9,8},{10,11... | collective-permute-start | bytes 2654216 | tf_op jit(solution)/shard_map/ppermute | solution.py:312
  165.1 4.5 %collective-permute-start.29 = (bf16[144,3072]{1,0:T(8,128)(2,1)S(1)}, bf16[144,3072]{1,0:T(8,128)(2,1)S(1)}, u32[]{:S(2)}, u32[]{:S(2)}) collective-permute-start(bf16[144,3072]{1,0:T(8,128)(2,1)S(1)} %get-tuple-element.50), channel_id=1, source_target_pairs={{0,1},{1,0},{2,3},{3,2},{4,5},{5,4},{6,7},{7,6},{8,9},{9,8},{10,11... | collective-permute-start | bytes 2654216 | tf_op jit(solution)/shard_map/ppermute | solution.py:312
  165.6 5.3 %collective-permute-start.24 = (bf16[144,3072]{1,0:T(8,128)(2,1)S(1)}, bf16[144,3072]{1,0:T(8,128)(2,1)S(1)}, u32[]{:S(2)}, u32[]{:S(2)}) collective-permute-start(bf16[144,3072]{1,0:T(8,128)(2,1)S(1)} %get-tuple-element.44), channel_id=1, source_target_pairs={{0,1},{1,0},{2,3},{3,2},{4,5},{5,4},{6,7},{7,6},{8,9},{9,8},{10,11... | collective-permute-start | bytes 2654216 | tf_op jit(solution)/shard_map/ppermute | solution.py:312
  165.6 7.6 %collective-permute-start.31 = (bf16[144,3072]{1,0:T(8,128)(2,1)S(1)}, bf16[144,3072]{1,0:T(8,128)(2,1)S(1)}, u32[]{:S(2)}, u32[]{:S(2)}) collective-permute-start(bf16[144,3072]{1,0:T(8,128)(2,1)S(1)} %collective-permute-done.22.refs_1_), channel_id=1, source_target_pairs={{0,1},{1,0},{2,3},{3,2},{4,5},{5,4},{6,7},{7,6},{8,9},{9,8},{10,11... | collective-permute-start | bytes 2654216 | tf_op jit(solution)/shard_map/ppermute | solution.py:307
  167.1 18.6 %collective-permute-start.32 = (bf16[144,3072]{1,0:T(8,128)(2,1)S(1)}, bf16[144,3072]{1,0:T(8,128)(2,1)S(1)}, u32[]{:S(2)}, u32[]{:S(2)}) collective-permute-start(bf16[144,3072]{1,0:T(8,128)(2,1)S(1)} %collective-permute-done.23.refs_2_), channel_id=1, source_target_pairs={{0,1},{1,0},{2,3},{3,2},{4,5},{5,4},{6,7},{7,6},{8,9},{9,8},{10,11... | collective-permute-start | bytes 2654216 | tf_op jit(solution)/shard_map/ppermute | solution.py:307
  171.1 15.6 %collective-permute-start.30 = (bf16[144,3072]{1,0:T(8,128)(2,1)S(1)}, bf16[144,3072]{1,0:T(8,128)(2,1)}, u32[]{:S(2)}, u32[]{:S(2)}) collective-permute-start(bf16[144,3072]{1,0:T(8,128)(2,1)S(1)} %collective-permute-done.21.refs_0_), channel_id=1, source_target_pairs={{0,1},{1,0},{2,3},{3,2},{4,5},{5,4},{6,7},{7,6},{8,9},{9,8},{10,11... | collective-permute-start | bytes 2654216 | tf_op jit(solution)/shard_map/ppermute | solution.py:307
  171.6 31.8 %collective-permute-start.39 = (bf16[144,3072]{1,0:T(8,128)(2,1)S(1)}, bf16[144,3072]{1,0:T(8,128)(2,1)S(1)}, u32[]{:S(2)}, u32[]{:S(2)}) collective-permute-start(bf16[144,3072]{1,0:T(8,128)(2,1)S(1)} %collective-permute-done.21.refs_0_), channel_id=1, source_target_pairs={{0,2},{2,0},{1,3},{3,1},{4,6},{6,4},{5,7},{7,5},{8,10},{10,8},{9,1... | collective-permute-start | bytes 2654216 | tf_op jit(solution)/shard_map/ppermute | solution.py:325
  173.2 30.1 %collective-permute-start.28 = (bf16[144,3072]{1,0:T(8,128)(2,1)S(1)}, bf16[144,3072]{1,0:T(8,128)(2,1)S(1)}, u32[]{:S(2)}, u32[]{:S(2)}) collective-permute-start(bf16[144,3072]{1,0:T(8,128)(2,1)S(1)} %add_convert_fusion.7), channel_id=1, source_target_pairs={{0,4},{4,8},{8,12},{12,0},{1,5},{5,9},{9,13},{13,1},{2,6},{6,10},{... | collective-permute-start | bytes 2654216 | tf_op jit(solution)/shard_map/ppermute | solution.py:318
  173.2 12.5 %copy-start.18 = (bf16[144,3072]{1,0:T(8,128)(2,1)}, bf16[144,3072]{1,0:T(8,128)(2,1)S(1)}, u32[]{:S(2)}) copy-start(bf16[144,3072]{1,0:T(8,128)(2,1)S(1)} %collective-permute-done.31.refs_4_) | copy-start | bytes 2654212
  173.2 31.0 %collective-permute-start.26 = (bf16[144,3072]{1,0:T(8,128)(2,1)S(1)}, bf16[144,3072]{1,0:T(8,128)(2,1)S(1)}, u32[]{:S(2)}, u32[]{:S(2)}) collective-permute-start(bf16[144,3072]{1,0:T(8,128)(2,1)S(1)} %add_convert_fusion.8), channel_id=1, source_target_pairs={{4,0},{8,4},{12,8},{0,12},{5,1},{9,5},{13,9},{1,13},{6,2},{10,6},{... | collective-permute-start | bytes 2654216 | tf_op jit(solution)/shard_map/ppermute | solution.py:318
  202.4 2.9 collective-permute-start.36
  203.2 3.3 %collective-permute-start.34 = (bf16[144,3072]{1,0:T(8,128)(2,1)S(1)}, bf16[144,3072]{1,0:T(8,128)(2,1)S(1)}, u32[]{:S(2)}, u32[]{:S(2)}) collective-permute-start(bf16[144,3072]{1,0:T(8,128)(2,1)S(1)} %get-tuple-element.55), channel_id=1, source_target_pairs={{0,1},{1,0},{2,3},{3,2},{4,5},{5,4},{6,7},{7,6},{8,9},{9,8},{10,11... | collective-permute-start | bytes 2654216 | tf_op jit(solution)/shard_map/ppermute | solution.py:312
  206.8 3.1 %collective-permute-start.40 = (bf16[144,3072]{1,0:T(8,128)(2,1)S(1)}, bf16[144,3072]{1,0:T(8,128)(2,1)S(1)}, u32[]{:S(2)}, u32[]{:S(2)}) collective-permute-start(bf16[144,3072]{1,0:T(8,128)(2,1)S(1)} %collective-permute-done.39.refs_0_), channel_id=1, source_target_pairs={{0,1},{1,0},{2,3},{3,2},{4,5},{5,4},{6,7},{7,6},{8,9},{9,8},{10,11... | collective-permute-start | bytes 2654216 | tf_op jit(solution)/shard_map/ppermute | solution.py:307
  207.2 14.6 %collective-permute-start.33 = (bf16[144,3072]{1,0:T(8,128)(2,1)S(1)}, bf16[144,3072]{1,0:T(8,128)(2,1)S(1)}, u32[]{:S(2)}, u32[]{:S(2)}) collective-permute-start(bf16[144,3072]{1,0:T(8,128)(2,1)S(1)} %get-tuple-element.53), channel_id=1, source_target_pairs={{0,1},{1,0},{2,3},{3,2},{4,5},{5,4},{6,7},{7,6},{8,9},{9,8},{10,11... | collective-permute-start | bytes 2654216 | tf_op jit(solution)/shard_map/ppermute | solution.py:312
  207.4 21.1 %collective-permute-start.35 = (bf16[144,3072]{1,0:T(8,128)(2,1)S(1)}, bf16[144,3072]{1,0:T(8,128)(2,1)S(1)}, u32[]{:S(2)}, u32[]{:S(2)}) collective-permute-start(bf16[144,3072]{1,0:T(8,128)(2,1)S(1)} %add_convert_fusion.4), channel_id=1, source_target_pairs={{4,0},{8,4},{12,8},{0,12},{5,1},{9,5},{13,9},{1,13},{6,2},{10,6},{... | collective-permute-start | bytes 2654216 | tf_op jit(solution)/shard_map/ppermute | solution.py:318
  209.9 21.6 %collective-permute-start.37 = (bf16[144,3072]{1,0:T(8,128)(2,1)S(1)}, bf16[144,3072]{1,0:T(8,128)(2,1)S(1)}, u32[]{:S(2)}, u32[]{:S(2)}) collective-permute-start(bf16[144,3072]{1,0:T(8,128)(2,1)S(1)} %add_convert_fusion.3), channel_id=1, source_target_pairs={{0,4},{4,8},{8,12},{12,0},{1,5},{5,9},{9,13},{13,1},{2,6},{6,10},{... | collective-permute-start | bytes 2654216 | tf_op jit(solution)/shard_map/ppermute | solution.py:318
  221.0 13.5 %collective-permute-start.41 = (bf16[144,3072]{1,0:T(8,128)(2,1)S(1)}, bf16[144,3072]{1,0:T(8,128)(2,1)S(1)}, u32[]{:S(2)}, u32[]{:S(2)}) collective-permute-start(bf16[144,3072]{1,0:T(8,128)(2,1)S(1)} %get-tuple-element.62), channel_id=1, source_target_pairs={{0,1},{1,0},{2,3},{3,2},{4,5},{5,4},{6,7},{7,6},{8,9},{9,8},{10,11... | collective-permute-start | bytes 2654216 | tf_op jit(solution)/shard_map/ppermute | solution.py:312
  231.5 21.3 %collective-permute-start.38 = (bf16[144,3072]{1,0:T(8,128)(2,1)}, bf16[144,3072]{1,0:T(8,128)(2,1)S(1)}, u32[]{:S(2)}, u32[]{:S(2)}) collective-permute-start(bf16[144,3072]{1,0:T(8,128)(2,1)} %add_convert_fusion.5), channel_id=1, source_target_pairs={{0,8},{4,12},{8,0},{12,4},{1,9},{5,13},{9,1},{13,5},{2,10},{6,14},... | collective-permute-start | bytes 2654216 | tf_op jit(solution)/shard_map/ppermute | solution.py:338
  232.9 6.8 %copy-start.5 = (bf16[32,6144]{1,0:T(8,128)(2,1)S(1)}, bf16[32,6144]{1,0:T(8,128)(2,1)}, u32[]{:S(2)}) copy-start(bf16[32,6144]{1,0:T(8,128)(2,1)} %copy-done.4) | copy-start | bytes 1179652
  232.9 21.3 %collective-permute-start.43 = (bf16[144,3072]{1,0:T(8,128)(2,1)}, bf16[144,3072]{1,0:T(8,128)(2,1)}, u32[]{:S(2)}, u32[]{:S(2)}) collective-permute-start(bf16[144,3072]{1,0:T(8,128)(2,1)} %add_convert_fusion.1), channel_id=1, source_target_pairs={{0,2},{2,0},{1,3},{3,1},{4,6},{6,4},{5,7},{7,5},{8,10},{10,8},{9,1... | collective-permute-start | bytes 2654216 | tf_op jit(solution)/shard_map/ppermute | solution.py:339
  235.6 39.9 %collective-permute-start.42 = (bf16[144,3072]{1,0:T(8,128)(2,1)}, bf16[144,3072]{1,0:T(8,128)(2,1)}, u32[]{:S(2)}, u32[]{:S(2)}) collective-permute-start(bf16[144,3072]{1,0:T(8,128)(2,1)} %add_convert_fusion.2), channel_id=1, source_target_pairs={{0,10},{2,8},{4,14},{6,12},{8,2},{10,0},{12,6},{14,4},{1,11},{3,9}... | collective-permute-start | bytes 2654216 | tf_op jit(solution)/shard_map/ppermute | solution.py:335
  279.9 18.5 %all-to-all-start.3 = ((bf16[8,18,3072]{2,1,0:T(8,128)(2,1)}), bf16[8,18,3072]{2,1,0:T(8,128)(2,1)S(1)}, u32[]{:S(2)}, u32[]{:S(2)}) async-start(bf16[8,18,3072]{2,1,0:T(8,128)(2,1)} %reshape.150), calls=%async_computation.3 | async-start | bytes 2359296 | tf_op jit(solution)/shard_map/all_to_all | solution.py:405
  283.5 3.8 %collective-permute-start.12 = (f32[32,2]{0,1:T(2,128)S(1)}, f32[32,2]{0,1:T(2,128)S(1)}, u32[]{:S(2)}, u32[]{:S(2)}) collective-permute-start(f32[32,2]{0,1:T(2,128)S(1)} %pad_maximum_fusion.4), channel_id=1, source_target_pairs={{0,1},{1,0},{2,3},{3,2},{4,5},{5,4},{6,7},{7,6},{8,9},{9,8},{10,11... | collective-permute-start | bytes 776 | tf_op jit(solution)/shard_map/ppermute | solution.py:397
  298.7 5.2 %copy-start.3 = (bf16[32,6144]{1,0:T(8,128)(2,1)S(1)}, bf16[32,6144]{1,0:T(8,128)(2,1)}, u32[]{:S(2)}) copy-start(bf16[32,6144]{1,0:T(8,128)(2,1)} %param.12) | copy-start | bytes 1179652
  299.3 4.6 %collective-permute-start.44 = (f32[32,3072]{1,0:T(8,128)S(1)}, f32[32,3072]{1,0:T(8,128)S(1)}, u32[]{:S(2)}, u32[]{:S(2)}) collective-permute-start(f32[32,3072]{1,0:T(8,128)S(1)} %get-tuple-element.64), channel_id=1, source_target_pairs={{0,1},{1,0},{2,3},{3,2},{4,5},{5,4},{6,7},{7,6},{8,9},{9,8},{10,11... | collective-permute-start | bytes 1179656 | tf_op jit(solution)/shard_map/ppermute | solution.py:411
  (10 other events, 19.8 us)
Sparse Core Ops, SparseCore 0:
  25.1 35.8 all-gather.1
